TPU v7x, 32 devices: a whole 2x2x4 slice. The times are simulated.
32 devices in a mesh: sec: 4 (over y, core), brick: 8 (over z, x).
Axes of the slice: x: 2, y: 2, z: 4, core: 2. Of those that a mesh axis runs over, the one named last changes fastest.
Arguments:
- potentials: float32 [4, 256, 32, 128], P('sec', 'brick'), may hold values from -0.3 to 1.2
- coefficient: float32 [4, 256, 32, 128], P('sec', 'brick'), may hold values from 0.04 to 0.32
- recovery: float32 [256, 32, 128], P('brick'), may hold values from 0 to 1
- excitable: int32 [256, 32, 128], P('brick'), may hold values 0 or 1
- row_of: int32 [8], P('brick'), may hold values from 0 to 2
Outputs:
- updated: float32 [4, 256, 32, 128], P('sec', 'brick')
Inputs may be any that keep to these rules, and one draw needn't show every extreme that they name: row_of[p] is the torso layer on which heart brick p lies.
All inputs are finite; a program needn't handle non-finite values. No bound on the sum of `excitable` on one device may be relied on, other than what follows from the above.
Results may differ from a plain program's by a relative error of at most 0.0003.
Values sent between devices are 32-bit elements; how exact they have to be, the bound alone decides.
A program may use at most 64 MiB of HBM per device.

v0:
```python
import jax
import jax.numpy as jnp
from jax import lax
from jax.sharding import PartitionSpec as P

SUBSTEPS = 8
SWEEPS = 16
STEPS = 2


coupling_gain = 0.1
ionic_timestep = 0.05
ionic_gain = 8.0
recovery_rate = 0.1
recovery_decay = 0.5
spectrum_low = 0.04
spectrum_high = 12.32
rim_depth = 4
heart_row = 3


def extended_2(value, sides, width):
    for axis, dim in sides:
        devices, length = (lax.axis_size(axis), value.shape[dim])
        up = [(i, (i + 1) % devices) for i in range(devices - 1)]
        down = [(j, i) for i, j in up]
        last = lax.slice_in_dim(value, length - width, length, axis=dim)
        initial = lax.slice_in_dim(value, 0, width, axis=dim)
        before = lax.ppermute(last, axis, up)
        after = lax.ppermute(initial, axis, down)
        value = jnp.concatenate([before, value, after], axis=dim)
    return value


def from_root(value, axis, root):
    mine = lax.axis_index(axis) == root
    return lax.psum(jnp.where(mine, value, jnp.zeros_like(value)), axis)


def chebyshev_weights(count):
    center = 0.5 * (spectrum_high + spectrum_low)
    spread = 0.5 * (spectrum_high - spectrum_low)
    ratio = center / spread
    current = 1.0 / ratio
    keeps = []
    pushes = []
    for number in range(count):
        following = 1.0 / (2.0 * ratio - current)
        keeps.append(following * current)
        pushes.append(2.0 * following / spread)
        current = following
    return (center, keeps, pushes)


def ionic(voltage, recovery, threshold, active):
    for substep in range(SUBSTEPS):
        drive = ionic_gain * voltage * (voltage - threshold) * (1.0 - voltage) - recovery
        relax = recovery_rate * (voltage - recovery_decay * recovery)
        voltage = voltage + ionic_timestep * active * drive
        recovery = recovery + ionic_timestep * active * relax
    return (voltage, recovery)


def keep_state(voltage, recovery, threshold, active):
    return (voltage, recovery)


def voltage_laplace(voltage, is_first, is_last):
    extended = extended_2(voltage, (("brick", 0),), 1)
    lower = jnp.where(is_first, voltage[:1], extended[:1])
    upper = jnp.where(is_last, voltage[-1:], extended[-1:])
    forward = jnp.concatenate([voltage[1:], upper], axis=0)
    backward = jnp.concatenate([lower, voltage[:-1]], axis=0)
    sides = jnp.pad(voltage, ((0, 0), (1, 1), (1, 1)), mode="edge")
    total = forward + backward
    total = total + sides[:, 2:, 1:-1] + sides[:, :-2, 1:-1]
    total = total + sides[:, 1:-1, 2:] + sides[:, 1:-1, :-2]
    return total - 6.0 * voltage


def beside_all(extended):
    inner = jnp.pad(extended[1:-1, 1:-1], ((0, 0), (0, 0), (1, 1)))
    total = extended[2:, 1:-1] + extended[:-2, 1:-1]
    total = total + extended[1:-1, 2:] + extended[1:-1, :-2]
    total = total + inner[:, :, 2:] + inner[:, :, :-2]
    return total


def deep_group(state, first, count, absorb_wide, inside_wide, keeps, pushes):
    iterate, direction, residual = state
    size_x = iterate.shape[0]
    size_y = iterate.shape[1]
    wide_dir, wide_res = (
        extended_2(direction, (("sec", 1), ("brick", 0)), rim_depth),
        extended_2(residual, (("sec", 1), ("brick", 0)), rim_depth),
    )
    depth = rim_depth
    for offset in range(count):
        iterate = iterate + wide_dir[depth : depth + size_x, depth : depth + size_y]
        start = rim_depth - depth + 1
        span_x = size_x + 2 * depth - 2
        span_y = size_y + 2 * depth - 2
        absorb = absorb_wide[start : start + span_x, start : start + span_y]
        inside = inside_wide[start : start + span_x, start : start + span_y]
        inner = wide_dir[1:-1, 1:-1]
        wide_res = (wide_res[1:-1, 1:-1] - ((6.0 + absorb) * inner - beside_all(wide_dir))) * inside
        wide_dir = keeps[first + offset] * inner + pushes[first + offset] * wide_res
        depth = depth - 1
    direction = wide_dir[depth : depth + size_x, depth : depth + size_y]
    residual = wide_res[depth : depth + size_x, depth : depth + size_y]
    return (iterate, direction, residual)


def body(potentials, coefficient, recovery, excitable, row_of):
    field = potentials[0]
    local_coef = coefficient[0]
    sec_index = lax.axis_index("sec")
    brick_index = lax.axis_index("brick")
    is_para = sec_index == heart_row
    scale = jnp.where(is_para, 0.0, 1.0).astype(jnp.float32)
    is_first = brick_index == 0
    is_last = brick_index == lax.axis_size("brick") - 1
    owner_row = row_of[0]
    owner = sec_index == owner_row
    active = excitable.astype(jnp.float32)
    voltage = field
    potential = field * scale
    center, keep_list, push_list = chebyshev_weights(SWEEPS - 1)
    keeps = jnp.array(keep_list, dtype=jnp.float32)
    pushes = jnp.array(push_list, dtype=jnp.float32)
    absorb_wide, inside_wide = (
        extended_2(local_coef, (("sec", 1), ("brick", 0)), rim_depth),
        extended_2(jnp.zeros_like(local_coef) + scale, (("sec", 1), ("brick", 0)), rim_depth),
    )
    source = voltage_laplace(voltage, is_first, is_last)
    for coupling_step in range(STEPS):
        extended = extended_2(potential, (("sec", 1), ("brick", 0)), 1)
        neighbours = beside_all(extended)
        current = neighbours - 6.0 * potential
        to_elliptic = from_root(source, "sec", heart_row)
        to_parabolic = from_root(current, "sec", owner_row)
        voltage, recovery = lax.cond(
            is_para, ionic, keep_state, voltage, recovery, local_coef, active
        )
        fresh = voltage_laplace(voltage, is_first, is_last)
        voltage = voltage + coupling_gain * (fresh + to_parabolic)
        placed = jnp.where(owner, to_elliptic, 0.0)
        residual = (placed - ((6.0 + local_coef) * potential - neighbours)) * scale
        direction = residual / center
        state = (potential, direction, residual)
        updates = SWEEPS - 1
        groups = updates // rim_depth
        rest = updates % rim_depth

        def run_group(group_number, carried):
            return deep_group(
                carried,
                group_number * rim_depth,
                rim_depth,
                absorb_wide,
                inside_wide,
                keeps,
                pushes,
            )

        state = lax.fori_loop(0, groups, run_group, state)
        state = deep_group(state, groups * rim_depth, rest, absorb_wide, inside_wide, keeps, pushes)
        potential = state[0] + state[1]
        source = fresh
    return jnp.where(is_para, voltage, potential)[None]


def solution(mesh):
    in_specs = (
        P("sec", "brick", None, None),
        P("sec", "brick", None, None),
        P("brick", None, None),
        P("brick", None, None),
        P("brick"),
    )
    out_specs = P("sec", "brick", None, None)
    return jax.shard_map(body, mesh=mesh, in_specs=in_specs, out_specs=out_specs, check_vma=False)
```

profile of v0, /device:TPU:0, one launch (start us, length us, event | category | flops | bytes accessed | tf_op | source)
XLA Modules:
  0.0 453.0 jit_solution(15722084760118619616)
XLA Ops:
  12.1 5.4 %collective-permute-start.25 = (f32[1,32,128]{2,1,0:T(8,128)}, f32[1,32,128]{2,1,0:T(8,128)}, u32[]{:S(2)}, u32[]{:S(2)}) collective-permute-start(f32[1,32,128]{2,1,0:T(8,128)} %get-tuple-element.803), channel_id=1, source_target_pairs={{0,1},{1,2},{2,3},{3,4},{4,5},{5,6},{6,7},{8,9},{9,10},{10,11},{11... | collective-permute-start | bytes 49160 | tf_op jit(solution)/shard_map/ppermute | solution.py:29
  29.0 5.8 %collective-permute-start.17 = (f32[1,32,128]{2,1,0:T(8,128)}, f32[1,32,128]{2,1,0:T(8,128)}, u32[]{:S(2)}, u32[]{:S(2)}) collective-permute-start(f32[1,32,128]{2,1,0:T(8,128)} %get-tuple-element.790), channel_id=1, source_target_pairs={{0,1},{1,2},{2,3},{3,4},{4,5},{5,6},{6,7},{8,9},{9,10},{10,11},{11... | collective-permute-start | bytes 49160 | tf_op jit(solution)/shard_map/ppermute | solution.py:29
  44.3 4.5 collective-permute-start.26
  48.9 4.3 collective-permute-start.21
  55.8 5.2 %collective-permute-start.28 = (f32[4,40,128]{2,1,0:T(8,128)S(1)}, f32[4,40,128]{2,1,0:T(8,128)S(1)}, u32[]{:S(2)}, u32[]{:S(2)}) collective-permute-start(f32[4,40,128]{2,1,0:T(8,128)S(1)} %get-tuple-element.765), channel_id=1, source_target_pairs={{0,1},{1,2},{2,3},{3,4},{4,5},{5,6},{6,7},{8,9},{9,10},{10,11},{11... | collective-permute-start | bytes 245768 | tf_op jit(solution)/shard_map/ppermute | solution.py:29
  62.4 5.4 %collective-permute-start.32 = (f32[4,40,128]{2,1,0:T(8,128)S(1)}, f32[4,40,128]{2,1,0:T(8,128)S(1)}, u32[]{:S(2)}, u32[]{:S(2)}) collective-permute-start(f32[4,40,128]{2,1,0:T(8,128)S(1)} %get-tuple-element.763), channel_id=1, source_target_pairs={{0,1},{1,2},{2,3},{3,4},{4,5},{5,6},{6,7},{8,9},{9,10},{10,11},{11... | collective-permute-start | bytes 245768 | tf_op jit(solution)/shard_map/ppermute | solution.py:29
  78.4 113.5 %while.42 = (s32[]{:T(128)}, f32[32,32,128]{2,1,0:T(8,128)}, f32[32,32,128]{2,1,0:T(8,128)S(1)}, f32[32,32,128]{2,1,0:T(8,128)S(1)}, f32[40,40,128]{2,1,0:T(8,12...) while((s32[]{:T(128)}, f32[32,32,128]{2,1,0:T(8,128)}, ...), condition=%wide.region_7.8_spmd.clone.clone, body=%wide.region_6.7_spmd.sunk.clone.clone.sunk | while | flops 10433554 | bytes 45280088 | solution.py:166
  90.4 4.6 %collective-permute-start.3 = (f32[4,40,128]{2,1,0:T(8,128)S(1)}, f32[4,40,128]{2,1,0:T(8,128)S(1)}, u32[]{:S(2)}, u32[]{:S(2)}) collective-permute-start(f32[4,40,128]{2,1,0:T(8,128)S(1)} %get-tuple-element.962), channel_id=1, source_target_pairs={{0,1},{1,2},{2,3},{3,4},{4,5},{5,6},{6,7},{8,9},{9,10},{10,11},{11... | collective-permute-start | bytes 245768 | tf_op jit(solution)/shard_map/while/body/eval_jaxpr/ppermute | solution.py:29
  96.3 5.3 %collective-permute-start.7 = (f32[4,40,128]{2,1,0:T(8,128)S(1)}, f32[4,40,128]{2,1,0:T(8,128)S(1)}, u32[]{:S(2)}, u32[]{:S(2)}) collective-permute-start(f32[4,40,128]{2,1,0:T(8,128)S(1)} %get-tuple-element.966), channel_id=1, source_target_pairs={{0,1},{1,2},{2,3},{3,4},{4,5},{5,6},{6,7},{8,9},{9,10},{10,11},{11... | collective-permute-start | bytes 245768 | tf_op jit(solution)/shard_map/while/body/eval_jaxpr/ppermute | solution.py:29
  122.2 4.0 collective-permute-start.5
  128.2 4.9 %collective-permute-start.3 = (f32[4,40,128]{2,1,0:T(8,128)S(1)}, f32[4,40,128]{2,1,0:T(8,128)S(1)}, u32[]{:S(2)}, u32[]{:S(2)}) collective-permute-start(f32[4,40,128]{2,1,0:T(8,128)S(1)} %get-tuple-element.962), channel_id=1, source_target_pairs={{0,1},{1,2},{2,3},{3,4},{4,5},{5,6},{6,7},{8,9},{9,10},{10,11},{11... | collective-permute-start | bytes 245768 | tf_op jit(solution)/shard_map/while/body/eval_jaxpr/ppermute | solution.py:29
  134.5 5.5 %collective-permute-start.7 = (f32[4,40,128]{2,1,0:T(8,128)S(1)}, f32[4,40,128]{2,1,0:T(8,128)S(1)}, u32[]{:S(2)}, u32[]{:S(2)}) collective-permute-start(f32[4,40,128]{2,1,0:T(8,128)S(1)} %get-tuple-element.966), channel_id=1, source_target_pairs={{0,1},{1,2},{2,3},{3,4},{4,5},{5,6},{6,7},{8,9},{9,10},{10,11},{11... | collective-permute-start | bytes 245768 | tf_op jit(solution)/shard_map/while/body/eval_jaxpr/ppermute | solution.py:29
  160.5 4.0 collective-permute-start.5
  166.5 4.9 %collective-permute-start.3 = (f32[4,40,128]{2,1,0:T(8,128)S(1)}, f32[4,40,128]{2,1,0:T(8,128)S(1)}, u32[]{:S(2)}, u32[]{:S(2)}) collective-permute-start(f32[4,40,128]{2,1,0:T(8,128)S(1)} %get-tuple-element.962), channel_id=1, source_target_pairs={{0,1},{1,2},{2,3},{3,4},{4,5},{5,6},{6,7},{8,9},{9,10},{10,11},{11... | collective-permute-start | bytes 245768 | tf_op jit(solution)/shard_map/while/body/eval_jaxpr/ppermute | solution.py:29
  172.8 5.5 %collective-permute-start.7 = (f32[4,40,128]{2,1,0:T(8,128)S(1)}, f32[4,40,128]{2,1,0:T(8,128)S(1)}, u32[]{:S(2)}, u32[]{:S(2)}) collective-permute-start(f32[4,40,128]{2,1,0:T(8,128)S(1)} %get-tuple-element.966), channel_id=1, source_target_pairs={{0,1},{1,2},{2,3},{3,4},{4,5},{5,6},{6,7},{8,9},{9,10},{10,11},{11... | collective-permute-start | bytes 245768 | tf_op jit(solution)/shard_map/while/body/eval_jaxpr/ppermute | solution.py:29
  197.6 4.0 collective-permute-start.38
  202.9 4.9 %collective-permute-start.36 = (f32[4,40,128]{2,1,0:T(8,128)S(1)}, f32[4,40,128]{2,1,0:T(8,128)S(1)}, u32[]{:S(2)}, u32[]{:S(2)}) collective-permute-start(f32[4,40,128]{2,1,0:T(8,128)S(1)} %get-tuple-element.761), channel_id=1, source_target_pairs={{0,1},{1,2},{2,3},{3,4},{4,5},{5,6},{6,7},{8,9},{9,10},{10,11},{11... | collective-permute-start | bytes 245768 | tf_op jit(solution)/shard_map/ppermute | solution.py:29
  209.2 5.6 %collective-permute-start.40 = (f32[4,40,128]{2,1,0:T(8,128)S(1)}, f32[4,40,128]{2,1,0:T(8,128)S(1)}, u32[]{:S(2)}, u32[]{:S(2)}) collective-permute-start(f32[4,40,128]{2,1,0:T(8,128)S(1)} %get-tuple-element.759), channel_id=1, source_target_pairs={{0,1},{1,2},{2,3},{3,4},{4,5},{5,6},{6,7},{8,9},{9,10},{10,11},{11... | collective-permute-start | bytes 245768 | tf_op jit(solution)/shard_map/ppermute | solution.py:29
  227.6 4.4 collective-permute-start.45
  234.6 4.4 collective-permute-done.44
  240.2 46.7 %all-reduce.22.cloned.1.call-done = (f32[32,32,128]{2,1,0:T(8,128)}, f32[32,32,128]{2,1,0:T(8,128)}, f32[32,32,128]{2,1,0:T(8,128)}) async-done(((f32[32,32,128]{2,1,0:T(8,128)}, f32[32,32,128]{2,1,0:T(8,128)}, f32[32,32,128]{2,1,0:T(8,128)}), (f32[32,32,128]{2,1,0:T(8,128)}, f32[32,32,128]{2,1,0:T(8,128)}, f32[32,32,128]{2,1,0:T(8,128)})) %all-reduce.22.cloned.1.call-update) | async-done | bytes 1572880 | tf_op jit(solution)/shard_map/psum | solution.py:37
  291.6 114.1 %while.43 = (s32[]{:T(128)}, f32[32,32,128]{2,1,0:T(8,128)}, f32[32,32,128]{2,1,0:T(8,128)S(1)}, f32[32,32,128]{2,1,0:T(8,128)S(1)}, f32[40,40,128]{2,1,0:T(8,12...) while((s32[]{:T(128)}, f32[32,32,128]{2,1,0:T(8,128)}, ...), condition=%wide.region_11.12_spmd.clone.clone, body=%wide.region_10.11_spmd.sunk.clone.clone.sunk | while | flops 10433554 | bytes 45280088 | solution.py:166
  304.1 4.6 %collective-permute-start.11 = (f32[4,40,128]{2,1,0:T(8,128)S(1)}, f32[4,40,128]{2,1,0:T(8,128)S(1)}, u32[]{:S(2)}, u32[]{:S(2)}) collective-permute-start(f32[4,40,128]{2,1,0:T(8,128)S(1)} %get-tuple-element.995), channel_id=1, source_target_pairs={{0,1},{1,2},{2,3},{3,4},{4,5},{5,6},{6,7},{8,9},{9,10},{10,11},{11... | collective-permute-start | bytes 245768 | tf_op jit(solution)/shard_map/while/body/eval_jaxpr/ppermute | solution.py:29
  310.0 4.9 %collective-permute-start.15 = (f32[4,40,128]{2,1,0:T(8,128)S(1)}, f32[4,40,128]{2,1,0:T(8,128)S(1)}, u32[]{:S(2)}, u32[]{:S(2)}) collective-permute-start(f32[4,40,128]{2,1,0:T(8,128)S(1)} %get-tuple-element.999), channel_id=1, source_target_pairs={{0,1},{1,2},{2,3},{3,4},{4,5},{5,6},{6,7},{8,9},{9,10},{10,11},{11... | collective-permute-start | bytes 245768 | tf_op jit(solution)/shard_map/while/body/eval_jaxpr/ppermute | solution.py:29
  341.6 5.0 %collective-permute-start.11 = (f32[4,40,128]{2,1,0:T(8,128)S(1)}, f32[4,40,128]{2,1,0:T(8,128)S(1)}, u32[]{:S(2)}, u32[]{:S(2)}) collective-permute-start(f32[4,40,128]{2,1,0:T(8,128)S(1)} %get-tuple-element.995), channel_id=1, source_target_pairs={{0,1},{1,2},{2,3},{3,4},{4,5},{5,6},{6,7},{8,9},{9,10},{10,11},{11... | collective-permute-start | bytes 245768 | tf_op jit(solution)/shard_map/while/body/eval_jaxpr/ppermute | solution.py:29
  348.0 5.5 %collective-permute-start.15 = (f32[4,40,128]{2,1,0:T(8,128)S(1)}, f32[4,40,128]{2,1,0:T(8,128)S(1)}, u32[]{:S(2)}, u32[]{:S(2)}) collective-permute-start(f32[4,40,128]{2,1,0:T(8,128)S(1)} %get-tuple-element.999), channel_id=1, source_target_pairs={{0,1},{1,2},{2,3},{3,4},{4,5},{5,6},{6,7},{8,9},{9,10},{10,11},{11... | collective-permute-start | bytes 245768 | tf_op jit(solution)/shard_map/while/body/eval_jaxpr/ppermute | solution.py:29
  374.2 4.0 collective-permute-start.13
  380.2 4.9 %collective-permute-start.11 = (f32[4,40,128]{2,1,0:T(8,128)S(1)}, f32[4,40,128]{2,1,0:T(8,128)S(1)}, u32[]{:S(2)}, u32[]{:S(2)}) collective-permute-start(f32[4,40,128]{2,1,0:T(8,128)S(1)} %get-tuple-element.995), channel_id=1, source_target_pairs={{0,1},{1,2},{2,3},{3,4},{4,5},{5,6},{6,7},{8,9},{9,10},{10,11},{11... | collective-permute-start | bytes 245768 | tf_op jit(solution)/shard_map/while/body/eval_jaxpr/ppermute | solution.py:29
  386.5 5.5 %collective-permute-start.15 = (f32[4,40,128]{2,1,0:T(8,128)S(1)}, f32[4,40,128]{2,1,0:T(8,128)S(1)}, u32[]{:S(2)}, u32[]{:S(2)}) collective-permute-start(f32[4,40,128]{2,1,0:T(8,128)S(1)} %get-tuple-element.999), channel_id=1, source_target_pairs={{0,1},{1,2},{2,3},{3,4},{4,5},{5,6},{6,7},{8,9},{9,10},{10,11},{11... | collective-permute-start | bytes 245768 | tf_op jit(solution)/shard_map/while/body/eval_jaxpr/ppermute | solution.py:29
  411.9 4.4 collective-permute-start.23
  424.2 5.8 %collective-permute-start.48 = (f32[4,40,128]{2,1,0:T(8,128)S(1)}, f32[4,40,128]{2,1,0:T(8,128)S(1)}, u32[]{:S(2)}, u32[]{:S(2)}) collective-permute-start(f32[4,40,128]{2,1,0:T(8,128)S(1)} %get-tuple-element.755), channel_id=1, source_target_pairs={{0,1},{1,2},{2,3},{3,4},{4,5},{5,6},{6,7},{8,9},{9,10},{10,11},{11... | collective-permute-start | bytes 245768 | tf_op jit(solution)/shard_map/ppermute | solution.py:29
  431.4 5.4 %collective-permute-start.52 = (f32[4,40,128]{2,1,0:T(8,128)S(1)}, f32[4,40,128]{2,1,0:T(8,128)S(1)}, u32[]{:S(2)}, u32[]{:S(2)}) collective-permute-start(f32[4,40,128]{2,1,0:T(8,128)S(1)} %get-tuple-element.753), channel_id=1, source_target_pairs={{0,1},{1,2},{2,3},{3,4},{4,5},{5,6},{6,7},{8,9},{9,10},{10,11},{11... | collective-permute-start | bytes 245768 | tf_op jit(solution)/shard_map/ppermute | solution.py:29
  (424 shorter events, 247.3 us)
Async XLA Ops:
  6.5 68.6 %all-reduce.20.cloned.1.call-start = ((), (), s32[]{:S(2)}) async-start(), calls=%async_computation | async-start | bytes 1048576 | tf_op jit(solution)/shard_map/psum | solution.py:37
  7.2 48.6 %collective-permute-start.31 = (f32[32,4,128]{2,1,0:T(4,128)}, f32[32,4,128]{2,1,0:T(4,128)S(1)}, u32[]{:S(2)}, u32[]{:S(2)}) collective-permute-start(f32[32,4,128]{2,1,0:T(4,128)} %slice.1526), channel_id=1, source_target_pairs={{8,0},{16,8},{24,16},{9,1},{17,9},{25,17},{10,2},{18,10},{26,18},{... | collective-permute-start | bytes 196616 | tf_op jit(solution)/shard_map/ppermute | solution.py:30
  8.5 52.6 %collective-permute-start.30 = (f32[32,4,128]{2,1,0:T(4,128)}, f32[32,4,128]{2,1,0:T(4,128)S(1)}, u32[]{:S(2)}, u32[]{:S(2)}) collective-permute-start(f32[32,4,128]{2,1,0:T(4,128)} %slice.1526), channel_id=1, source_target_pairs={{0,8},{8,16},{16,24},{1,9},{9,17},{17,25},{2,10},{10,18},{18,26},{... | collective-permute-start | bytes 196616 | tf_op jit(solution)/shard_map/ppermute | solution.py:29
  12.1 16.8 %collective-permute-start.25 = (f32[1,32,128]{2,1,0:T(8,128)}, f32[1,32,128]{2,1,0:T(8,128)}, u32[]{:S(2)}, u32[]{:S(2)}) collective-permute-start(f32[1,32,128]{2,1,0:T(8,128)} %get-tuple-element.803), channel_id=1, source_target_pairs={{0,1},{1,2},{2,3},{3,4},{4,5},{5,6},{6,7},{8,9},{9,10},{10,11},{11... | collective-permute-start | bytes 49160 | tf_op jit(solution)/shard_map/ppermute | solution.py:29
  17.6 17.2 %collective-permute-start.24 = (f32[1,32,128]{2,1,0:T(8,128)}, f32[1,32,128]{2,1,0:T(8,128)}, u32[]{:S(2)}, u32[]{:S(2)}) collective-permute-start(f32[1,32,128]{2,1,0:T(8,128)} %get-tuple-element.804), channel_id=1, source_target_pairs={{1,0},{2,1},{3,2},{4,3},{5,4},{6,5},{7,6},{9,8},{10,9},{11,10},{12... | collective-permute-start | bytes 49160 | tf_op jit(solution)/shard_map/ppermute | solution.py:30
  27.7 12.7 %collective-permute-start.16 = (f32[1,32,128]{2,1,0:T(8,128)}, f32[1,32,128]{2,1,0:T(8,128)}, u32[]{:S(2)}, u32[]{:S(2)}) collective-permute-start(f32[1,32,128]{2,1,0:T(8,128)} %get-tuple-element.789), channel_id=1, source_target_pairs={{1,0},{2,1},{3,2},{4,3},{5,4},{6,5},{7,6},{9,8},{10,9},{11,10},{12... | collective-permute-start | bytes 49160 | tf_op jit(solution)/shard_map/ppermute | solution.py:30
  29.0 12.7 %collective-permute-start.17 = (f32[1,32,128]{2,1,0:T(8,128)}, f32[1,32,128]{2,1,0:T(8,128)}, u32[]{:S(2)}, u32[]{:S(2)}) collective-permute-start(f32[1,32,128]{2,1,0:T(8,128)} %get-tuple-element.790), channel_id=1, source_target_pairs={{0,1},{1,2},{2,3},{3,4},{4,5},{5,6},{6,7},{8,9},{9,10},{10,11},{11... | collective-permute-start | bytes 49160 | tf_op jit(solution)/shard_map/ppermute | solution.py:29
  38.1 248.9 %all-reduce.22.cloned.1.call-start = ((), (), s32[]{:S(2)}) async-start(), calls=%async_computation.1 | async-start | bytes 3145728 | tf_op jit(solution)/shard_map/psum | solution.py:37
  48.9 24.4 %collective-permute-start.21 = (f32[1,34,128]{2,1,0:T(8,128)S(1)}, f32[1,34,128]{2,1,0:T(8,128)S(1)}, u32[]{:S(2)}, u32[]{:S(2)}) collective-permute-start(f32[1,34,128]{2,1,0:T(8,128)S(1)} %get-tuple-element.772), channel_id=1, source_target_pairs={{0,1},{1,2},{2,3},{3,4},{4,5},{5,6},{6,7},{8,9},{9,10},{10,11},{11... | collective-permute-start | bytes 52232 | tf_op jit(solution)/shard_map/ppermute | solution.py:29
  53.2 20.1 %collective-permute-start.20 = (f32[1,34,128]{2,1,0:T(8,128)S(1)}, f32[1,34,128]{2,1,0:T(8,128)S(1)}, u32[]{:S(2)}, u32[]{:S(2)}) collective-permute-start(f32[1,34,128]{2,1,0:T(8,128)S(1)} %get-tuple-element.771), channel_id=1, source_target_pairs={{1,0},{2,1},{3,2},{4,3},{5,4},{6,5},{7,6},{9,8},{10,9},{11,10},{12... | collective-permute-start | bytes 52232 | tf_op jit(solution)/shard_map/ppermute | solution.py:30
  55.8 12.1 %collective-permute-start.28 = (f32[4,40,128]{2,1,0:T(8,128)S(1)}, f32[4,40,128]{2,1,0:T(8,128)S(1)}, u32[]{:S(2)}, u32[]{:S(2)}) collective-permute-start(f32[4,40,128]{2,1,0:T(8,128)S(1)} %get-tuple-element.765), channel_id=1, source_target_pairs={{0,1},{1,2},{2,3},{3,4},{4,5},{5,6},{6,7},{8,9},{9,10},{10,11},{11... | collective-permute-start | bytes 245768 | tf_op jit(solution)/shard_map/ppermute | solution.py:29
  89.1 12.5 %collective-permute-start.2 = (f32[4,40,128]{2,1,0:T(8,128)S(1)}, f32[4,40,128]{2,1,0:T(8,128)S(1)}, u32[]{:S(2)}, u32[]{:S(2)}) collective-permute-start(f32[4,40,128]{2,1,0:T(8,128)S(1)} %get-tuple-element.961), channel_id=1, source_target_pairs={{1,0},{2,1},{3,2},{4,3},{5,4},{6,5},{7,6},{9,8},{10,9},{11,10},{12... | collective-permute-start | bytes 245768 | tf_op jit(solution)/shard_map/while/body/eval_jaxpr/ppermute | solution.py:30
  120.9 12.3 %collective-permute-start.4 = (f32[32,4,128]{2,1,0:T(4,128)}, f32[32,4,128]{2,1,0:T(4,128)S(1)}, u32[]{:S(2)}, u32[]{:S(2)}) collective-permute-start(f32[32,4,128]{2,1,0:T(4,128)} %get-tuple-element.963), channel_id=1, source_target_pairs={{8,0},{16,8},{24,16},{9,1},{17,9},{25,17},{10,2},{18,10},{26,18},{... | collective-permute-start | bytes 196616 | tf_op jit(solution)/shard_map/while/body/eval_jaxpr/ppermute | solution.py:30
  126.9 13.1 %collective-permute-start.2 = (f32[4,40,128]{2,1,0:T(8,128)S(1)}, f32[4,40,128]{2,1,0:T(8,128)S(1)}, u32[]{:S(2)}, u32[]{:S(2)}) collective-permute-start(f32[4,40,128]{2,1,0:T(8,128)S(1)} %get-tuple-element.961), channel_id=1, source_target_pairs={{1,0},{2,1},{3,2},{4,3},{5,4},{6,5},{7,6},{9,8},{10,9},{11,10},{12... | collective-permute-start | bytes 245768 | tf_op jit(solution)/shard_map/while/body/eval_jaxpr/ppermute | solution.py:30
  128.2 11.8 %collective-permute-start.3 = (f32[4,40,128]{2,1,0:T(8,128)S(1)}, f32[4,40,128]{2,1,0:T(8,128)S(1)}, u32[]{:S(2)}, u32[]{:S(2)}) collective-permute-start(f32[4,40,128]{2,1,0:T(8,128)S(1)} %get-tuple-element.962), channel_id=1, source_target_pairs={{0,1},{1,2},{2,3},{3,4},{4,5},{5,6},{6,7},{8,9},{9,10},{10,11},{11... | collective-permute-start | bytes 245768 | tf_op jit(solution)/shard_map/while/body/eval_jaxpr/ppermute | solution.py:29
  159.2 12.3 %collective-permute-start.4 = (f32[32,4,128]{2,1,0:T(4,128)}, f32[32,4,128]{2,1,0:T(4,128)S(1)}, u32[]{:S(2)}, u32[]{:S(2)}) collective-permute-start(f32[32,4,128]{2,1,0:T(4,128)} %get-tuple-element.963), channel_id=1, source_target_pairs={{8,0},{16,8},{24,16},{9,1},{17,9},{25,17},{10,2},{18,10},{26,18},{... | collective-permute-start | bytes 196616 | tf_op jit(solution)/shard_map/while/body/eval_jaxpr/ppermute | solution.py:30
  165.2 13.1 %collective-permute-start.2 = (f32[4,40,128]{2,1,0:T(8,128)S(1)}, f32[4,40,128]{2,1,0:T(8,128)S(1)}, u32[]{:S(2)}, u32[]{:S(2)}) collective-permute-start(f32[4,40,128]{2,1,0:T(8,128)S(1)} %get-tuple-element.961), channel_id=1, source_target_pairs={{1,0},{2,1},{3,2},{4,3},{5,4},{6,5},{7,6},{9,8},{10,9},{11,10},{12... | collective-permute-start | bytes 245768 | tf_op jit(solution)/shard_map/while/body/eval_jaxpr/ppermute | solution.py:30
  166.5 11.8 %collective-permute-start.3 = (f32[4,40,128]{2,1,0:T(8,128)S(1)}, f32[4,40,128]{2,1,0:T(8,128)S(1)}, u32[]{:S(2)}, u32[]{:S(2)}) collective-permute-start(f32[4,40,128]{2,1,0:T(8,128)S(1)} %get-tuple-element.962), channel_id=1, source_target_pairs={{0,1},{1,2},{2,3},{3,4},{4,5},{5,6},{6,7},{8,9},{9,10},{10,11},{11... | collective-permute-start | bytes 245768 | tf_op jit(solution)/shard_map/while/body/eval_jaxpr/ppermute | solution.py:29
  201.6 13.2 %collective-permute-start.37 = (f32[4,40,128]{2,1,0:T(8,128)S(1)}, f32[4,40,128]{2,1,0:T(8,128)S(1)}, u32[]{:S(2)}, u32[]{:S(2)}) collective-permute-start(f32[4,40,128]{2,1,0:T(8,128)S(1)} %get-tuple-element.762), channel_id=1, source_target_pairs={{1,0},{2,1},{3,2},{4,3},{5,4},{6,5},{7,6},{9,8},{10,9},{11,10},{12... | collective-permute-start | bytes 245768 | tf_op jit(solution)/shard_map/ppermute | solution.py:30
  202.9 12.0 %collective-permute-start.36 = (f32[4,40,128]{2,1,0:T(8,128)S(1)}, f32[4,40,128]{2,1,0:T(8,128)S(1)}, u32[]{:S(2)}, u32[]{:S(2)}) collective-permute-start(f32[4,40,128]{2,1,0:T(8,128)S(1)} %get-tuple-element.761), channel_id=1, source_target_pairs={{0,1},{1,2},{2,3},{3,4},{4,5},{5,6},{6,7},{8,9},{9,10},{10,11},{11... | collective-permute-start | bytes 245768 | tf_op jit(solution)/shard_map/ppermute | solution.py:29
  302.8 12.1 %collective-permute-start.10 = (f32[4,40,128]{2,1,0:T(8,128)S(1)}, f32[4,40,128]{2,1,0:T(8,128)S(1)}, u32[]{:S(2)}, u32[]{:S(2)}) collective-permute-start(f32[4,40,128]{2,1,0:T(8,128)S(1)} %get-tuple-element.994), channel_id=1, source_target_pairs={{1,0},{2,1},{3,2},{4,3},{5,4},{6,5},{7,6},{9,8},{10,9},{11,10},{12... | collective-permute-start | bytes 245768 | tf_op jit(solution)/shard_map/while/body/eval_jaxpr/ppermute | solution.py:30
  334.4 12.3 %collective-permute-start.12 = (f32[32,4,128]{2,1,0:T(4,128)}, f32[32,4,128]{2,1,0:T(4,128)S(1)}, u32[]{:S(2)}, u32[]{:S(2)}) collective-permute-start(f32[32,4,128]{2,1,0:T(4,128)} %get-tuple-element.996), channel_id=1, source_target_pairs={{8,0},{16,8},{24,16},{9,1},{17,9},{25,17},{10,2},{18,10},{26,18},{... | collective-permute-start | bytes 196616 | tf_op jit(solution)/shard_map/while/body/eval_jaxpr/ppermute | solution.py:30
  340.3 13.1 %collective-permute-start.10 = (f32[4,40,128]{2,1,0:T(8,128)S(1)}, f32[4,40,128]{2,1,0:T(8,128)S(1)}, u32[]{:S(2)}, u32[]{:S(2)}) collective-permute-start(f32[4,40,128]{2,1,0:T(8,128)S(1)} %get-tuple-element.994), channel_id=1, source_target_pairs={{1,0},{2,1},{3,2},{4,3},{5,4},{6,5},{7,6},{9,8},{10,9},{11,10},{12... | collective-permute-start | bytes 245768 | tf_op jit(solution)/shard_map/while/body/eval_jaxpr/ppermute | solution.py:30
  341.6 11.9 %collective-permute-start.11 = (f32[4,40,128]{2,1,0:T(8,128)S(1)}, f32[4,40,128]{2,1,0:T(8,128)S(1)}, u32[]{:S(2)}, u32[]{:S(2)}) collective-permute-start(f32[4,40,128]{2,1,0:T(8,128)S(1)} %get-tuple-element.995), channel_id=1, source_target_pairs={{0,1},{1,2},{2,3},{3,4},{4,5},{5,6},{6,7},{8,9},{9,10},{10,11},{11... | collective-permute-start | bytes 245768 | tf_op jit(solution)/shard_map/while/body/eval_jaxpr/ppermute | solution.py:29
  372.9 12.3 %collective-permute-start.12 = (f32[32,4,128]{2,1,0:T(4,128)}, f32[32,4,128]{2,1,0:T(4,128)S(1)}, u32[]{:S(2)}, u32[]{:S(2)}) collective-permute-start(f32[32,4,128]{2,1,0:T(4,128)} %get-tuple-element.996), channel_id=1, source_target_pairs={{8,0},{16,8},{24,16},{9,1},{17,9},{25,17},{10,2},{18,10},{26,18},{... | collective-permute-start | bytes 196616 | tf_op jit(solution)/shard_map/while/body/eval_jaxpr/ppermute | solution.py:30
  378.9 13.1 %collective-permute-start.10 = (f32[4,40,128]{2,1,0:T(8,128)S(1)}, f32[4,40,128]{2,1,0:T(8,128)S(1)}, u32[]{:S(2)}, u32[]{:S(2)}) collective-permute-start(f32[4,40,128]{2,1,0:T(8,128)S(1)} %get-tuple-element.994), channel_id=1, source_target_pairs={{1,0},{2,1},{3,2},{4,3},{5,4},{6,5},{7,6},{9,8},{10,9},{11,10},{12... | collective-permute-start | bytes 245768 | tf_op jit(solution)/shard_map/while/body/eval_jaxpr/ppermute | solution.py:30
  380.2 11.8 %collective-permute-start.11 = (f32[4,40,128]{2,1,0:T(8,128)S(1)}, f32[4,40,128]{2,1,0:T(8,128)S(1)}, u32[]{:S(2)}, u32[]{:S(2)}) collective-permute-start(f32[4,40,128]{2,1,0:T(8,128)S(1)} %get-tuple-element.995), channel_id=1, source_target_pairs={{0,1},{1,2},{2,3},{3,4},{4,5},{5,6},{6,7},{8,9},{9,10},{10,11},{11... | collective-permute-start | bytes 245768 | tf_op jit(solution)/shard_map/while/body/eval_jaxpr/ppermute | solution.py:29
  405.7 17.2 %collective-permute-start.47 = (f32[32,4,128]{2,1,0:T(4,128)S(1)}, f32[32,4,128]{2,1,0:T(4,128)S(1)}, u32[]{:S(2)}, u32[]{:S(2)}) collective-permute-start(f32[32,4,128]{2,1,0:T(4,128)S(1)} %get-tuple-element.784), channel_id=1, source_target_pairs={{8,0},{16,8},{24,16},{9,1},{17,9},{25,17},{10,2},{18,10},{26,18},{... | collective-permute-start | bytes 196616 | tf_op jit(solution)/shard_map/ppermute | solution.py:30
  407.0 15.9 %collective-permute-start.46 = (f32[32,4,128]{2,1,0:T(4,128)S(1)}, f32[32,4,128]{2,1,0:T(4,128)S(1)}, u32[]{:S(2)}, u32[]{:S(2)}) collective-permute-start(f32[32,4,128]{2,1,0:T(4,128)S(1)} %get-tuple-element.783), channel_id=1, source_target_pairs={{0,8},{8,16},{16,24},{1,9},{9,17},{17,25},{2,10},{10,18},{18,26},{... | collective-permute-start | bytes 196616 | tf_op jit(solution)/shard_map/ppermute | solution.py:29
  417.6 12.4 %collective-permute-start.51 = (f32[32,4,128]{2,1,0:T(4,128)S(1)}, f32[32,4,128]{2,1,0:T(4,128)S(1)}, u32[]{:S(2)}, u32[]{:S(2)}) collective-permute-start(f32[32,4,128]{2,1,0:T(4,128)S(1)} %get-tuple-element.782), channel_id=1, source_target_pairs={{8,0},{16,8},{24,16},{9,1},{17,9},{25,17},{10,2},{18,10},{26,18},{... | collective-permute-start | bytes 196616 | tf_op jit(solution)/shard_map/ppermute | solution.py:30
  422.9 14.0 %collective-permute-start.49 = (f32[4,40,128]{2,1,0:T(8,128)S(1)}, f32[4,40,128]{2,1,0:T(8,128)S(1)}, u32[]{:S(2)}, u32[]{:S(2)}) collective-permute-start(f32[4,40,128]{2,1,0:T(8,128)S(1)} %get-tuple-element.756), channel_id=1, source_target_pairs={{1,0},{2,1},{3,2},{4,3},{5,4},{6,5},{7,6},{9,8},{10,9},{11,10},{12... | collective-permute-start | bytes 245768 | tf_op jit(solution)/shard_map/ppermute | solution.py:30
  424.2 12.7 %collective-permute-start.48 = (f32[4,40,128]{2,1,0:T(8,128)S(1)}, f32[4,40,128]{2,1,0:T(8,128)S(1)}, u32[]{:S(2)}, u32[]{:S(2)}) collective-permute-start(f32[4,40,128]{2,1,0:T(8,128)S(1)} %get-tuple-element.755), channel_id=1, source_target_pairs={{0,1},{1,2},{2,3},{3,4},{4,5},{5,6},{6,7},{8,9},{9,10},{10,11},{11... | collective-permute-start | bytes 245768 | tf_op jit(solution)/shard_map/ppermute | solution.py:29
  (117 other events, 801.9 us)
Sparse Core Ops, SparseCore 0:
  38.2 36.8 all-reduce.19
  240.3 46.5 all-reduce.21
where the time goes:
time: 458 us; the launch traced here: 453 us
  starting transfers between devices  239 us (52%)
  waiting for transfers between devices  82.3 us (18%)
  other arithmetic  75 us (16%)
  local copies, waits for them, and re-layouts  39.9 us (9%)
  between operations  15.3 us (3%)
    ppermute x43, starting transfers between devices, extended_2(): before = lax.ppermute(last, axis, up)  184 us
    ppermute x43, starting transfers between devices, extended_2(): after = lax.ppermute(initial, axis, down)  55.4 us
    add x28, other arithmetic, deep_group(): wide_dir = keeps[first + offset] * inner + pushes[first + offset] * wide_res  52.4 us
    psum x2, waiting for transfers between devices, from_root(): return lax.psum(jnp.where(mine, value, jnp.zeros_like(value)), axis)  48.6 us
    ppermute x43, waiting for transfers between devices, extended_2(): before = lax.ppermute(last, axis, up)  25 us
    while x24, local copies, waits for them, and re-layouts  10.5 us
    slice x18, local copies, waits for them, and re-layouts, extended_2(): last = lax.slice_in_dim(value, length - width, length, axis=dim)  9.36 us
  transfers between devices with their start and end apart: 88, of which 22 were waited for; matrix products, arithmetic and copies ran while one was open for 7% of the time, Pallas kernels for 0%

commit v1 on v0

v1 whole, which is shorter than its diff:
```python
import functools

import jax
import jax.numpy as jnp
import numpy as np
from jax import lax
from jax.experimental import pallas as pl
from jax.experimental.pallas import tpu as pltpu
from jax.sharding import PartitionSpec as P

SUBSTEPS = 8
SWEEPS = 16
STEPS = 2
GROUPS = SWEEPS // 2

coupling_gain = 0.1
ionic_timestep = 0.05
ionic_gain = 8.0
recovery_rate = 0.1
recovery_decay = 0.5
spectrum_low = 0.04
spectrum_high = 12.32

center = 0.5 * (spectrum_high + spectrum_low)
spread = 0.5 * (spectrum_high - spectrum_low)
back = (0.5 * spread) ** 2


def push_weights():
    ratio = center / spread
    values = [1.0, ratio]
    while len(values) <= SWEEPS:
        values.append(2.0 * ratio * values[-1] - values[-2])
    return [(0.5 * spread) ** k * values[k] for k in range(SWEEPS + 1)]


PUSHES = push_weights()
FINAL = 1.0 / PUSHES[SWEEPS]
MESH = pl.DeviceIdType.MESH
PAD = 8
DIAGONAL = ((0, 0), (0, 1), (1, 0), (1, 1))


def largest_divisor(count, limit):
    return max(u for u in range(1, limit + 1) if count % u == 0)


def for_planes(first, count, limit, work):
    unroll = largest_divisor(count, limit)

    def chunk(i, carry):
        done = [work(first + i * unroll + j) for j in range(unroll)]
        for value, store in done:
            store(value)
        return carry

    lax.fori_loop(0, count // unroll, chunk, 0)


def kernel(sections, bricks, pot, coef, rec, exc, push, row, out,
           A, B, EB, GB, BB, JA, JB, W, T, M, HX, HY, HC, SY, SC, R, R2, ER, SE, BR, PR, VH,
           lsem, xsend, xrecv, isend, irecv, gsend, grecv, jsend, jrecv, vsend, vrecv):
    X, Y, Z = W.shape
    sec = lax.axis_index("sec")
    brick = lax.axis_index("brick")
    heart = sections - 1
    is_heart = sec == heart
    has_x = (brick > 0, brick < bricks - 1)
    to_x = (brick - 1, brick + 1)
    has_y = (jnp.logical_and(sec > 0, sec < heart), sec < heart - 1)
    to_y = (sec - 1, sec + 1)
    rows = pl.ds(PAD, Y)
    lane = lax.broadcasted_iota(jnp.int32, (Y, Z), 1)
    lane_x = lax.broadcasted_iota(jnp.int32, (X, Z), 1)

    def remote(src, dst, send, recv, s, b):
        return pltpu.make_async_remote_copy(
            src_ref=src, dst_ref=dst, send_sem=send, recv_sem=recv,
            device_id={"sec": s, "brick": b}, device_id_type=MESH)

    field = pltpu.make_async_copy(pot.at[0], A.at[pl.ds(2, X), rows], lsem.at[0])
    second = pltpu.make_async_copy(coef.at[0], T, lsem.at[1])
    field.start()
    second.start()

    barrier = pltpu.get_barrier_semaphore()

    @pl.when(jnp.logical_not(is_heart))
    def _():
        def clear(i, carry):
            for buf in (A, B):
                buf[i, 0:PAD, :] = jnp.zeros((PAD, Z), jnp.float32)
                buf[i, pl.ds(PAD + Y, PAD), :] = jnp.zeros((PAD, Z), jnp.float32)
            return carry

        lax.fori_loop(0, X + 4, clear, 0)
        for buf in (HX, HY, HC, ER, R2):
            buf[...] = jnp.zeros(buf.shape, jnp.float32)
        EB[0] = jnp.zeros((Y, Z), jnp.float32)
        EB[X + 1] = jnp.zeros((Y, Z), jnp.float32)
        PR[...] = jnp.full(PR.shape, -1.0, jnp.float32)

    for d in range(1, sections):
        pl.semaphore_signal(barrier, inc=1, device_id={"sec": lax.rem(sec + d, sections)},
                            device_id_type=MESH)
    total = sections - 1
    for i in range(2):
        @pl.when(has_x[i])
        def _():
            pl.semaphore_signal(barrier, inc=1, device_id={"sec": sec, "brick": to_x[i]},
                                device_id_type=MESH)
        total = total + has_x[i].astype(jnp.int32)
    for i, j in DIAGONAL:
        both = jnp.logical_and(has_x[i], has_y[j])

        @pl.when(both)
        def _():
            pl.semaphore_signal(barrier, inc=1, device_id={"sec": to_y[j], "brick": to_x[i]},
                                device_id_type=MESH)
        total = total + both.astype(jnp.int32)
    pl.semaphore_wait(barrier, total)
    field.wait()

    def heart_program():
        recover = pltpu.make_async_copy(rec, W, lsem.at[2])
        excite = pltpu.make_async_copy(exc, M, lsem.at[3])
        recover.start()
        excite.start()

        def sides(round_number):
            for i in range(2):
                src = A.at[pl.ds(2, 2) if i == 0 else pl.ds(X, 2), rows]

                @pl.when(has_x[i])
                def _():
                    remote(src, VH.at[round_number, 1 - i], vsend.at[i],
                           vrecv.at[round_number, 1 - i], sec, to_x[i]).start()
            for i in range(2):
                src = A.at[pl.ds(2, 2) if i == 0 else pl.ds(X, 2), rows]
                at = 0 if i == 0 else X + 2

                @pl.when(has_x[i])
                def _():
                    got = remote(src, VH.at[round_number, i], vsend.at[i],
                                 vrecv.at[round_number, i], sec, to_x[i])
                    got.wait_recv()
                    got.wait_send()
                    for j in range(2):
                        A[at + j, rows, :] = VH[round_number, i, j]

                @pl.when(jnp.logical_not(has_x[i]))
                def _():
                    for j in range(2):
                        A[at + j, rows, :] = A[2 if i == 0 else X + 1, rows, :]

            def edge(i, carry):
                A[i, pl.ds(PAD - 1, 1), :] = A[i, pl.ds(PAD, 1), :]
                A[i, pl.ds(PAD + Y, 1), :] = A[i, pl.ds(PAD + Y - 1, 1), :]
                return carry

            lax.fori_loop(0, X + 4, edge, 0)

        def laplace(x):
            c = A[x + 2, rows, :]
            total = A[x + 1, rows, :] + A[x + 3, rows, :]
            total = total + A[x + 2, pl.ds(PAD - 1, Y), :] + A[x + 2, pl.ds(PAD + 1, Y), :]
            total = total + jnp.where(lane == 0, c, pltpu.roll(c, 1, 1))
            total = total + jnp.where(lane == Z - 1, c, pltpu.roll(c, Z - 1, 1))
            return total - 6.0 * c

        def ionic(x):
            v = A[x + 2, rows, :]
            w = W[x]
            thresh = T[x]
            active = ionic_timestep * M[x].astype(jnp.float32)
            for _ in range(SUBSTEPS):
                drive = ionic_gain * v * (v - thresh) * (1.0 - v) - w
                relax = recovery_rate * (v - recovery_decay * w)
                v = v + active * drive
                w = w + active * relax

            def store(value):
                A[x + 2, rows, :] = value[0]
                W[x] = value[1]
            return (v, w), store

        def source(step):
            def work(x):
                def store(value):
                    GB[step, x + 1] = value
                return laplace(x), store
            for_planes(-1, X + 2, 4, work)
            for n in range(2):
                remote(GB.at[step], GB.at[step], gsend.at[step, n], grecv.at[step],
                       heart - 1 - n, brick).start()

        def current(step):
            for n in range(2):
                remote(JB.at[step, n], JB.at[step, n], jsend.at[step], jrecv.at[step, n],
                       heart - 1 - n, brick).wait_recv()

        sides(0)
        source(0)
        second.wait()
        recover.wait()
        excite.wait()
        for step in range(STEPS):
            for_planes(0, X, 2, ionic)
            sides(step + 1)
            if step + 1 < STEPS:
                source(step + 1)
                current(step)

                def advance(x):
                    def store(value):
                        A[x + 2, rows, :] = value
                    gain = GB[step + 1, x + 1] + (JB[step, 0, x] + JB[step, 1, x])
                    return A[x + 2, rows, :] + coupling_gain * gain, store
                for_planes(0, X, 4, advance)
            else:
                def before(x):
                    def store(value):
                        BB[x] = value
                    return A[x + 2, rows, :] + coupling_gain * laplace(x), store
                for_planes(0, X, 4, before)
                current(step)

                def final(x):
                    def store(value):
                        out[0, x] = value
                    return BB[x] + coupling_gain * (JB[step, 0, x] + JB[step, 1, x]), store
                for_planes(0, X, 4, final)
        for step in range(STEPS):
            for n in range(2):
                remote(GB.at[step], GB.at[step], gsend.at[step, n], grecv.at[step],
                       heart - 1 - n, brick).wait_send()

    def torso_program():
        one = jnp.ones((), jnp.float32)
        zero = jnp.zeros((), jnp.float32)
        inside_x = [jnp.where(h, one, zero) for h in has_x]
        inside_y = [jnp.where(h, one, zero) for h in has_y]
        section = sec.astype(jnp.float32)
        own = jnp.where(row[...] == section, 1.0, 0.0)
        own_y = (jnp.where(row[...] == section - 1.0, 1.0, 0.0),
                 jnp.where(row[...] == section + 1.0, 1.0, 0.0))

        def messages(slot):
            found = []
            for i in range(2):
                found.append((has_x[i], A.at[pl.ds(2, 2) if i == 0 else pl.ds(X, 2), rows],
                              HX.at[slot, 1 - i], HX.at[slot, i], 1 - i, i, sec, to_x[i]))
            for j in range(2):
                found.append((has_y[j], SY.at[j], HY.at[slot, 1 - j], HY.at[slot, j],
                              3 - j, 2 + j, to_y[j], brick))
            for n, (i, j) in enumerate(DIAGONAL):
                found.append((jnp.logical_and(has_x[i], has_y[j]), SC.at[n], HC.at[slot, 3 - n],
                              HC.at[slot, n], 7 - n, 4 + n, to_y[j], to_x[i]))
            return found

        def send_all(slot):
            for there, src, dst, land, far, near, s, b in messages(slot):
                @pl.when(there)
                def _():
                    remote(src, dst, xsend.at[near], xrecv.at[slot, far], s, b).start()

        def wait_all(slot, sent):
            for there, src, dst, land, far, near, s, b in messages(slot):
                @pl.when(there)
                def _():
                    got = remote(src, land, xsend.at[near], xrecv.at[slot, near], s, b)
                    if sent:
                        got.wait_send()
                    else:
                        got.wait_recv()

        def pack():
            def one_plane(x, carry):
                for j in range(2):
                    for n in range(2):
                        at = PAD + n if j == 0 else PAD + Y - 1 - n
                        SY[j, n, pl.ds(x, 1), :] = A[x + 2, pl.ds(at, 1), :]
                return carry
            lax.fori_loop(0, X, one_plane, 0, unroll=True)
            for n, (i, j) in enumerate(DIAGONAL):
                SC[n, 0:1, :] = A[2 if i == 0 else X + 1, pl.ds(PAD if j == 0 else PAD + Y - 1, 1), :]

        def stencil(src, x):
            c = src[x + 2, rows, :]
            total = src[x + 1, rows, :] + src[x + 3, rows, :]
            total = total + (src[x + 2, pl.ds(PAD - 1, Y), :] + src[x + 2, pl.ds(PAD + 1, Y), :])
            total = total + (jnp.where(lane == 0, 0.0, pltpu.roll(c, 1, 1))
                             + jnp.where(lane == Z - 1, 0.0, pltpu.roll(c, Z - 1, 1)))
            return total + EB[x + 1] * c

        def plane(src, dst, first, weight):
            def work(x):
                value = stencil(src, x)
                if first:
                    value = 0.5 * value
                else:
                    value = (value + weight * BB[x + 1]) - back * dst[x + 2, rows, :]

                def store(value):
                    dst[x + 2, rows, :] = value
                return value, store
            return work

        def mend(dst, low, high, halo, offset, scale):
            def one_plane(x, carry):
                for j, at in ((0, PAD), (1, PAD + Y - 1)):
                    dst[x + 2, pl.ds(at, 1), :] = (dst[x + 2, pl.ds(at, 1), :]
                                                   + scale * halo[j, pl.ds(x + offset, 1), :])
                return carry
            lax.fori_loop(low, high, one_plane, 0, unroll=True)

        def fringe(slot, first, weight):
            for j in range(2):
                c = R[j, pl.ds(PAD, X), :]
                total = R[j, pl.ds(PAD - 1, X), :] + R[j, pl.ds(PAD + 1, X), :]
                total = total + SY[j, 0] + HY[slot, j, 1]
                total = total + jnp.where(lane_x == 0, 0.0, pltpu.roll(c, 1, 1))
                total = total + jnp.where(lane_x == Z - 1, 0.0, pltpu.roll(c, Z - 1, 1))
                total = total + ER[j] * c
                if first:
                    R2[j] = (0.5 * inside_y[j]) * total
                else:
                    R2[j] = inside_y[j] * (total + weight * BR[j] - back * R2[j])

        def landed(slot):
            for j in range(2):
                A[j, rows, :] = HX[slot, 0, j]
                A[X + 2 + j, rows, :] = HX[slot, 1, j]
                R[j, pl.ds(PAD, X), :] = HY[slot, j, 0]
            for n, (i, j) in enumerate(DIAGONAL):
                R[j, pl.ds(PAD - 1 if i == 0 else PAD + X, 1), :] = HC[slot, n, 0:1, :]

        def edges(first, weight):
            for x in (-1, 0, X - 1, X):
                value, store = plane(A, B, first, weight)(x)
                store(value)

        def close_edges():
            B[1, rows, :] = inside_x[0] * B[1, rows, :]
            B[X + 2, rows, :] = inside_x[1] * B[X + 2, rows, :]

        def relay_source(step):
            return remote(GB.at[step], GB.at[step], gsend.at[step, 2], grecv.at[step],
                          heart - 3, brick)

        def wait_source(step):
            remote(GB.at[step], GB.at[step], gsend.at[step, 2], grecv.at[step],
                   heart, brick).wait_recv()

        def current_copy(step):
            inner = sec == heart - 3
            target = jnp.where(inner, heart - 2, heart)
            place = jnp.where(sec == heart - 2, 1, 0)
            return remote(JA.at[step], JB.at[step, place], jsend.at[step], jrecv.at[step, place],
                          target, brick)

        def init_copies():
            found = []
            for i in range(2):
                found.append((has_x[i], EB.at[1 if i == 0 else X], EB.at[X + 1 if i == 0 else 0],
                              EB.at[0 if i == 0 else X + 1], 1 - i, i, sec, to_x[i]))
                found.append((has_x[i], row, PR.at[1 - i], PR.at[i], 5 - i, 4 + i, sec, to_x[i]))
            for j in range(2):
                found.append((has_y[j], SE.at[j], ER.at[1 - j], ER.at[j], 3 - j, 2 + j,
                              to_y[j], brick))
            return found

        def set_up():
            second.wait()

            def absorb(x):
                def store(value):
                    EB[x + 1] = value
                return (center - 6.0) - T[x], store
            for_planes(0, X, 4, absorb)

            def one_plane(x, carry):
                SE[0, pl.ds(x, 1), :] = EB[x + 1, 0:1, :]
                SE[1, pl.ds(x, 1), :] = EB[x + 1, pl.ds(Y - 1, 1), :]
                return carry
            lax.fori_loop(0, X, one_plane, 0, unroll=True)
            for there, src, dst, land, far, near, s, b in init_copies():
                @pl.when(there)
                def _():
                    remote(src, dst, isend.at[near], irecv.at[far], s, b).start()

        def step_body(step, carry):
            pack()
            send_all(0)

            @pl.when(step == 0)
            def _():
                set_up()
            for_planes(1, X - 2, 6, plane(A, B, True, None))
            wait_all(0, False)

            @pl.when(step == 0)
            def _():
                for there, src, dst, land, far, near, s, b in init_copies():
                    @pl.when(there)
                    def _():
                        got = remote(src, land, isend.at[near], irecv.at[near], s, b)
                        got.wait_recv()
                        got.wait_send()
            landed(0)
            edges(True, None)
            fringe(0, True, None)
            mend(B, -1, X + 1, R, PAD, 0.5)
            close_edges()

            def current(x):
                def store(value):
                    JA[step, x] = value
                own_v = jnp.broadcast_to(own[0:1], (Y, Z))
                value = 2.0 * B[x + 2, rows, :] - (EB[x + 1] + 6.0) * A[x + 2, rows, :]
                return own_v * value, store
            for_planes(0, X, 4, current)

            @pl.when(sec != heart - 2)
            def _():
                current_copy(step).start()

            @pl.when(jnp.logical_or(sec != heart - 2, step == 0))
            def _():
                wait_source(step)

            @pl.when(jnp.logical_and(sec == heart - 2, step == 0))
            def _():
                relay_source(step).start()

            flags = [jnp.where(PR[i] == section, 1.0, 0.0) for i in range(2)]

            def place(flag):
                def work(x):
                    value = jnp.broadcast_to(flag[0:1], (Y, Z)) * GB[step, x + 1]

                    def store(value):
                        BB[x + 1] = value
                        B[x + 2, rows, :] = B[x + 2, rows, :] + 0.5 * value
                    return value, store
                return work
            for_planes(0, X, 4, place(own))
            for x, flag in ((-1, flags[0]), (X, flags[1])):
                value, store = place(flag)(x)
                store(value)

            def source_rows(x, carry):
                BR[0, pl.ds(x, 1), :] = own_y[0][0:1] * GB[step, x + 1, pl.ds(Y - 1, 1), :]
                BR[1, pl.ds(x, 1), :] = own_y[1][0:1] * GB[step, x + 1, pl.ds(0, 1), :]
                return carry
            lax.fori_loop(0, X, source_rows, 0, unroll=True)
            for j in range(2):
                R2[j] = R2[j] + 0.5 * BR[j]
            wait_all(0, True)
            for_planes(0, X, 8, plane(B, A, False, push[1]))
            mend(A, 0, X, R2, 0, 1.0)

            def group(g, carry):
                slot = lax.rem(g, 2)
                pack()
                send_all(slot)

                @pl.when(jnp.logical_and(g == 1, sec == heart - 2))
                def _():
                    remote(JB.at[step, 0], JB.at[step, 0], jsend.at[step], jrecv.at[step, 0],
                           heart, brick).wait_recv()

                    def add(x):
                        def store(value):
                            JA[step, x] = value
                        return JA[step, x] + JB[step, 0, x], store
                    for_planes(0, X, 4, add)
                    current_copy(step).start()

                @pl.when(jnp.logical_and(jnp.logical_and(g == GROUPS - 3, step + 1 < STEPS),
                                         sec == heart - 2))
                def _():
                    wait_source(step + 1)
                    relay_source(step + 1).start()

                first = push[2 * g]
                for_planes(1, X - 2, 6, plane(A, B, False, first))
                wait_all(slot, False)
                landed(slot)
                edges(False, first)
                fringe(slot, False, first)
                mend(B, -1, X + 1, R, PAD, 1.0)
                close_edges()
                wait_all(slot, True)
                for_planes(0, X, 8, plane(B, A, False, push[2 * g + 1]))
                mend(A, 0, X, R2, 0, 1.0)
                return carry

            lax.fori_loop(1, GROUPS, group, 0)

            def scale(x):
                def store(value):
                    A[x + 2, rows, :] = value
                return FINAL * A[x + 2, rows, :], store
            for_planes(0, X, 8, scale)
            return carry

        lax.fori_loop(0, STEPS, step_body, 0)

        def write(x):
            def store(value):
                out[0, x] = value
            return A[x + 2, rows, :], store
        for_planes(0, X, 8, write)
        for step in range(STEPS):
            current_copy(step).wait_send()

            @pl.when(sec == heart - 2)
            def _():
                relay_source(step).wait_send()

    pl.when(is_heart)(heart_program)
    pl.when(jnp.logical_not(is_heart))(torso_program)


def body(mesh, potentials, coefficient, recovery, excitable, row_of):
    sections, bricks = mesh.shape["sec"], mesh.shape["brick"]
    _, X, Y, Z = potentials.shape
    row = jnp.broadcast_to(row_of.astype(jnp.float32)[:, None], (8, Z))
    f32 = jnp.float32
    scratch = [
        ((X + 4, Y + 2 * PAD, Z), f32), ((X + 4, Y + 2 * PAD, Z), f32),
        ((X + 2, Y, Z), f32), ((STEPS, X + 2, Y, Z), f32), ((X + 2, Y, Z), f32),
        ((STEPS, X, Y, Z), f32), ((STEPS, 2, X, Y, Z), f32),
        ((X, Y, Z), f32), ((X, Y, Z), f32), ((X, Y, Z), jnp.int32),
        ((2, 2, 2, Y, Z), f32), ((2, 2, 2, X, Z), f32), ((2, 4, 8, Z), f32),
        ((2, 2, X, Z), f32), ((4, 8, Z), f32),
        ((2, X + 2 * PAD, Z), f32), ((2, X, Z), f32),
        ((2, X, Z), f32), ((2, X, Z), f32), ((2, X, Z), f32),
        ((2, 8, Z), f32), ((STEPS + 1, 2, 2, Y, Z), f32),
    ]
    sems = [(4,), (8,), (2, 8), (6,), (6,), (STEPS, 3), (STEPS,), (STEPS,), (STEPS, 2),
            (2,), (STEPS + 1, 2)]
    vmem = pl.BlockSpec(memory_space=pltpu.VMEM)
    anywhere = pl.BlockSpec(memory_space=pl.ANY)
    cells = X * Y * Z
    return pl.pallas_call(
        functools.partial(kernel, sections, bricks),
        out_shape=jax.ShapeDtypeStruct(potentials.shape, f32),
        in_specs=[anywhere] * 4 + [pl.BlockSpec(memory_space=pltpu.SMEM), vmem],
        out_specs=vmem,
        scratch_shapes=[pltpu.VMEM(s, t) for s, t in scratch]
        + [pltpu.SemaphoreType.DMA(s) for s in sems],
        compiler_params=pltpu.CompilerParams(
            collective_id=0, has_side_effects=True, vmem_limit_bytes=40 * 2**20),
        cost_estimate=pl.CostEstimate(
            flops=cells * STEPS * SWEEPS * 12, bytes_accessed=20 * cells, transcendentals=0),
    )(potentials, coefficient, recovery, excitable, jnp.asarray(np.array(PUSHES, np.float32)), row)


def solution(mesh):
    in_specs = (
        P("sec", "brick", None, None),
        P("sec", "brick", None, None),
        P("brick", None, None),
        P("brick", None, None),
        P("brick"),
    )
    out_specs = P("sec", "brick", None, None)
    return jax.shard_map(functools.partial(body, mesh), mesh=mesh, in_specs=in_specs,
                         out_specs=out_specs, check_vma=False)
```

time: 458 us -> 94.6 us (0.21)
  starting transfers between devices: 239 us -> 0 us
  Pallas kernels: 0 us -> 87.4 us
  waiting for transfers between devices: 82.3 us -> 0 us
  other arithmetic: 75 us -> 0 us
  local copies, waits for them, and re-layouts: 39.9 us -> 5.6 us
  between operations: 15.3 us -> 0.68 us
    ppermute x86 -> x0, starting transfers between devices: 239 us -> none  [the longest x43 184 us: extended_2(): before = lax.ppermute(last, axis, up)]
    pallas_call x0 -> x1, Pallas kernels: none -> 87.4 us  [body(): pl.pallas_call(functools.partial(kernel, sections, bricks), out_shape=jax...]
    add x33 -> x0, other arithmetic: 56.2 us -> none  [the longest x28 52.4 us: deep_group(): wide_dir = keeps[first + offset] * inner + pushes[first + offset] * wide_res]
    psum x2 -> x0, waiting for transfers between devices: 48.6 us -> none  [from_root(): return lax.psum(jnp.where(mine, value, jnp.zeros_like(value)), axis)]
    ppermute x86 -> x0, waiting for transfers between devices: 33.7 us -> none  [the longest x43 25 us: extended_2(): before = lax.ppermute(last, axis, up)]
    slice x65 -> x0, local copies, waits for them, and re-layouts: 20.6 us -> none  [the longest x18 9.36 us: extended_2(): last = lax.slice_in_dim(value, length - width, length, axis=dim)]
    while x24 -> x0, local copies, waits for them, and re-layouts: 10.5 us -> none
    select_n x7 -> x0, other arithmetic: 8.62 us -> none  [the longest x4 6.54 us: from_root(): return lax.psum(jnp.where(mine, value, jnp.zeros_like(value)), axis)]
  transfers between devices with their start and end apart: 88 -> 0, of which waited for: 22 -> 0; matrix products, arithmetic and copies ran while one was open for 7% -> 0% of each run, Pallas kernels for 0% -> 0%
where the time goes in v1:
time: 94.6 us; the launch traced here: 93.7 us
  Pallas kernels  87.4 us (92%)
  local copies, waits for them, and re-layouts  5.6 us (6%)
    pallas_call x1, Pallas kernels, body(): pl.pallas_call(functools.partial(kernel, sections, bricks), out_shape=jax...  87.4 us
    unnamed x11, local copies, waits for them, and re-layouts  5.6 us

profile of v1, /device:TPU:0, one launch (start us, length us, event | category | flops | bytes accessed | tf_op | source)
XLA Modules:
  0.0 93.7 jit_solution(3724541223971229298)
XLA Ops:
  0.7 0.0 copy-start.4
  0.7 0.6 copy-done.4
  1.3 0.0 copy-start
  1.3 1.0 %copy-done = f32[1,32,32,128]{3,2,1,0:T(8,128)S(1)} copy-done((f32[1,32,32,128]{3,2,1,0:T(8,128)S(1)}, f32[1,32,32,128]{3,2,1,0:T(8,128)}, u32[]{:S(2)}) %copy-start) | copy-done | bytes 524312
  2.4 0.0 copy-start.1
  2.4 1.0 %copy-done.1 = f32[1,32,32,128]{3,2,1,0:T(8,128)S(1)} copy-done((f32[1,32,32,128]{3,2,1,0:T(8,128)S(1)}, f32[1,32,32,128]{3,2,1,0:T(8,128)}, u32[]{:S(2)}) %copy-start.1) | copy-done | bytes 524312
  3.4 0.0 copy-start.2
  3.4 1.0 %copy-done.2 = f32[32,32,128]{2,1,0:T(8,128)S(1)} copy-done((f32[32,32,128]{2,1,0:T(8,128)S(1)}, f32[32,32,128]{2,1,0:T(8,128)}, u32[]{:S(2)}) %copy-start.2) | copy-done | bytes 524312
  4.4 0.0 copy-start.3
  4.4 1.0 %copy-done.3 = s32[32,32,128]{2,1,0:T(8,128)S(1)} copy-done((s32[32,32,128]{2,1,0:T(8,128)S(1)}, s32[32,32,128]{2,1,0:T(8,128)}, u32[]{:S(2)}) %copy-start.3) | copy-done | bytes 524312
  5.5 87.4 %shard_map.64 = f32[1,32,32,128]{3,2,1,0:T(8,128)S(1)} custom-call(f32[1,32,32,128]{3,2,1,0:T(8,128)S(1)} %copy-done, f32[1,32,32,128]{3,2,1,0:T(8,128)S(1)} %copy-done.1, f32[32,32,128]{2,1,0:T(8,128)S(1)} %copy-done.2, s32[32,32,128]{2,1,0:T(8,128)S(1)} %copy-done.3, f32[17]{0:T(128)S(1)} %copy-done.4, f32[8,128]{1,0:T(8,128)S(1)} %broadcast_in_dim.9.row), custom_call_target="tpu_custom_call" | custom-call | flops 50331648 | bytes 2621440 | tf_op jit(solution)/shard_map/pallas_call | solution.py:547
  92.9 0.8 copy.9
  (1 shorter events, 0.0 us)
Async XLA Ops:
  0.7 0.7 copy-start.4
  1.3 1.0 %copy-start = (f32[1,32,32,128]{3,2,1,0:T(8,128)S(1)}, f32[1,32,32,128]{3,2,1,0:T(8,128)}, u32[]{:S(2)}) copy-start(f32[1,32,32,128]{3,2,1,0:T(8,128)} %pot.1) | copy-start | bytes 1572868
  2.4 1.0 %copy-start.1 = (f32[1,32,32,128]{3,2,1,0:T(8,128)S(1)}, f32[1,32,32,128]{3,2,1,0:T(8,128)}, u32[]{:S(2)}) copy-start(f32[1,32,32,128]{3,2,1,0:T(8,128)} %coef.1) | copy-start | bytes 1572868
  3.4 1.0 %copy-start.2 = (f32[32,32,128]{2,1,0:T(8,128)S(1)}, f32[32,32,128]{2,1,0:T(8,128)}, u32[]{:S(2)}) copy-start(f32[32,32,128]{2,1,0:T(8,128)} %rec.1) | copy-start | bytes 1572868
  4.4 1.0 %copy-start.3 = (s32[32,32,128]{2,1,0:T(8,128)S(1)}, s32[32,32,128]{2,1,0:T(8,128)}, u32[]{:S(2)}) copy-start(s32[32,32,128]{2,1,0:T(8,128)} %exc.1) | copy-start | bytes 1572868

commit v2 on v1

--- a/solution.py
+++ b/solution.py
@@ -2,7 +2,6 @@
 
 import jax
 import jax.numpy as jnp
-import numpy as np
 from jax import lax
 from jax.experimental import pallas as pl
 from jax.experimental.pallas import tpu as pltpu
@@ -31,11 +30,11 @@
     values = [1.0, ratio]
     while len(values) <= SWEEPS:
         values.append(2.0 * ratio * values[-1] - values[-2])
-    return [(0.5 * spread) ** k * values[k] for k in range(SWEEPS + 1)]
+    grown = [(0.5 * spread) ** k * values[k] for k in range(SWEEPS + 1)]
+    return grown[:SWEEPS] + [1.0] * (GROUPS - 1) + [1.0 / grown[SWEEPS]]
 
 
 PUSHES = push_weights()
-FINAL = 1.0 / PUSHES[SWEEPS]
 MESH = pl.DeviceIdType.MESH
 PAD = 8
 DIAGONAL = ((0, 0), (0, 1), (1, 0), (1, 1))
@@ -57,8 +56,8 @@
     lax.fori_loop(0, count // unroll, chunk, 0)
 
 
-def kernel(sections, bricks, pot, coef, rec, exc, push, row, out,
-           A, B, EB, GB, BB, JA, JB, W, T, M, HX, HY, HC, SY, SC, R, R2, ER, SE, BR, PR, VH,
+def kernel(sections, bricks, pot, coef, rec, exc, row_of, out,
+           A, B, EB, GB, BB, JA, JB, W, T, M, HX, HY, HC, SY, SC, R, R2, ER, SE, BR, PR, VH, row, push,
            lsem, xsend, xrecv, isend, irecv, gsend, grecv, jsend, jrecv, vsend, vrecv):
     X, Y, Z = W.shape
     sec = lax.axis_index("sec")
@@ -73,11 +72,16 @@
     lane = lax.broadcasted_iota(jnp.int32, (Y, Z), 1)
     lane_x = lax.broadcasted_iota(jnp.int32, (X, Z), 1)
 
+    def across(buf, at, first, count, pitch):
+        return buf.reshape(buf.size // Z, Z), pl.ds(first * pitch + at, count, stride=pitch)
+
     def remote(src, dst, send, recv, s, b):
         return pltpu.make_async_remote_copy(
             src_ref=src, dst_ref=dst, send_sem=send, recv_sem=recv,
             device_id={"sec": s, "brick": b}, device_id_type=MESH)
 
+    for n, value in enumerate(PUSHES):
+        push[n] = jnp.float32(value)
     field = pltpu.make_async_copy(pot.at[0], A.at[pl.ds(2, X), rows], lsem.at[0])
     second = pltpu.make_async_copy(coef.at[0], T, lsem.at[1])
     field.start()
@@ -99,6 +103,7 @@
         EB[0] = jnp.zeros((Y, Z), jnp.float32)
         EB[X + 1] = jnp.zeros((Y, Z), jnp.float32)
         PR[...] = jnp.full(PR.shape, -1.0, jnp.float32)
+        row[...] = jnp.full(row.shape, row_of[0].astype(jnp.float32), jnp.float32)
 
     for d in range(1, sections):
         pl.semaphore_signal(barrier, inc=1, device_id={"sec": lax.rem(sec + d, sections)},
@@ -121,13 +126,22 @@
     pl.semaphore_wait(barrier, total)
     field.wait()
 
+    cuts = largest_divisor(X - 2, 3)
+    size = (X - 2) // cuts
+    parts = [(2 + n * size, size) for n in range(cuts)] + [(0, 2), (X, 2)]
+    inner, outer = range(cuts), range(cuts, cuts + 2)
+
+    def source_copy(step, n, lane_number, target):
+        ref = GB.at[step, pl.ds(parts[n][0], parts[n][1])]
+        return remote(ref, ref, gsend.at[step, n, lane_number], grecv.at[step, n], target, brick)
+
     def heart_program():
         recover = pltpu.make_async_copy(rec, W, lsem.at[2])
         excite = pltpu.make_async_copy(exc, M, lsem.at[3])
         recover.start()
         excite.start()
 
-        def sides(round_number):
+        def send_sides(round_number):
             for i in range(2):
                 src = A.at[pl.ds(2, 2) if i == 0 else pl.ds(X, 2), rows]
 
@@ -135,6 +149,8 @@
                 def _():
                     remote(src, VH.at[round_number, 1 - i], vsend.at[i],
                            vrecv.at[round_number, 1 - i], sec, to_x[i]).start()
+
+        def sides(round_number):
             for i in range(2):
                 src = A.at[pl.ds(2, 2) if i == 0 else pl.ds(X, 2), rows]
                 at = 0 if i == 0 else X + 2
@@ -153,12 +169,16 @@
                     for j in range(2):
                         A[at + j, rows, :] = A[2 if i == 0 else X + 1, rows, :]
 
+            edge_rows(0, 2)
+            edge_rows(X + 2, X + 4)
+
+        def edge_rows(low, high):
             def edge(i, carry):
                 A[i, pl.ds(PAD - 1, 1), :] = A[i, pl.ds(PAD, 1), :]
                 A[i, pl.ds(PAD + Y, 1), :] = A[i, pl.ds(PAD + Y - 1, 1), :]
                 return carry
 
-            lax.fori_loop(0, X + 4, edge, 0)
+            lax.fori_loop(low, high, edge, 0)
 
         def laplace(x):
             c = A[x + 2, rows, :]
@@ -184,31 +204,37 @@
                 W[x] = value[1]
             return (v, w), store
 
-        def source(step):
+        def source(step, chunks):
             def work(x):
                 def store(value):
                     GB[step, x + 1] = value
                 return laplace(x), store
-            for_planes(-1, X + 2, 4, work)
-            for n in range(2):
-                remote(GB.at[step], GB.at[step], gsend.at[step, n], grecv.at[step],
-                       heart - 1 - n, brick).start()
+            for n in chunks:
+                low, count = parts[n]
+                for_planes(low - 1, count, 5, work)
+                for far in (2, 1):
+                    source_copy(step, n, far - 1, heart - far).start()
 
         def current(step):
             for n in range(2):
                 remote(JB.at[step, n], JB.at[step, n], jsend.at[step], jrecv.at[step, n],
                        heart - 1 - n, brick).wait_recv()
 
+        edge_rows(2, X + 2)
+        send_sides(0)
+        source(0, inner)
         sides(0)
-        source(0)
+        source(0, outer)
         second.wait()
         recover.wait()
         excite.wait()
         for step in range(STEPS):
             for_planes(0, X, 2, ionic)
+            send_sides(step + 1)
+            edge_rows(2, X + 2)
             sides(step + 1)
             if step + 1 < STEPS:
-                source(step + 1)
+                source(step + 1, range(len(parts)))
                 current(step)
 
                 def advance(x):
@@ -231,9 +257,9 @@
                     return BB[x] + coupling_gain * (JB[step, 0, x] + JB[step, 1, x]), store
                 for_planes(0, X, 4, final)
         for step in range(STEPS):
-            for n in range(2):
-                remote(GB.at[step], GB.at[step], gsend.at[step, n], grecv.at[step],
-                       heart - 1 - n, brick).wait_send()
+            for n in range(len(parts)):
+                for far in (2, 1):
+                    source_copy(step, n, far - 1, heart - far).wait_send()
 
     def torso_program():
         one = jnp.ones((), jnp.float32)
@@ -258,9 +284,9 @@
                               HC.at[slot, n], 7 - n, 4 + n, to_y[j], to_x[i]))
             return found
 
-        def send_all(slot):
-            for there, src, dst, land, far, near, s, b in messages(slot):
-                @pl.when(there)
+        def send(slot, which, more):
+            for there, src, dst, land, far, near, s, b in [messages(slot)[n] for n in which]:
+                @pl.when(jnp.logical_and(there, more))
                 def _():
                     remote(src, dst, xsend.at[near], xrecv.at[slot, far], s, b).start()
 
@@ -274,14 +300,14 @@
                     else:
                         got.wait_recv()
 
-        def pack():
-            def one_plane(x, carry):
-                for j in range(2):
-                    for n in range(2):
-                        at = PAD + n if j == 0 else PAD + Y - 1 - n
-                        SY[j, n, pl.ds(x, 1), :] = A[x + 2, pl.ds(at, 1), :]
-                return carry
-            lax.fori_loop(0, X, one_plane, 0, unroll=True)
+        def pack_rows():
+            for j in range(2):
+                for n in range(2):
+                    at = PAD + n if j == 0 else PAD + Y - 1 - n
+                    flat, where = across(A, at, 2, X, Y + 2 * PAD)
+                    SY[j, n] = flat[where, :]
+
+        def pack_corners():
             for n, (i, j) in enumerate(DIAGONAL):
                 SC[n, 0:1, :] = A[2 if i == 0 else X + 1, pl.ds(PAD if j == 0 else PAD + Y - 1, 1), :]
 
@@ -293,13 +319,15 @@
                              + jnp.where(lane == Z - 1, 0.0, pltpu.roll(c, Z - 1, 1)))
             return total + EB[x + 1] * c
 
-        def plane(src, dst, first, weight):
+        def plane(src, dst, first, weight, scale=None):
             def work(x):
                 value = stencil(src, x)
                 if first:
                     value = 0.5 * value
                 else:
                     value = (value + weight * BB[x + 1]) - back * dst[x + 2, rows, :]
+                if scale is not None:
+                    value = scale * value
 
                 def store(value):
                     dst[x + 2, rows, :] = value
@@ -307,12 +335,9 @@
             return work
 
         def mend(dst, low, high, halo, offset, scale):
-            def one_plane(x, carry):
-                for j, at in ((0, PAD), (1, PAD + Y - 1)):
-                    dst[x + 2, pl.ds(at, 1), :] = (dst[x + 2, pl.ds(at, 1), :]
-                                                   + scale * halo[j, pl.ds(x + offset, 1), :])
-                return carry
-            lax.fori_loop(low, high, one_plane, 0, unroll=True)
+            for j, at in ((0, PAD), (1, PAD + Y - 1)):
+                flat, where = across(dst, at, low + 2, high - low, Y + 2 * PAD)
+                flat[where, :] = flat[where, :] + scale * halo[j, pl.ds(low + offset, high - low), :]
 
         def fringe(slot, first, weight):
             for j in range(2):
@@ -344,13 +369,11 @@
             B[1, rows, :] = inside_x[0] * B[1, rows, :]
             B[X + 2, rows, :] = inside_x[1] * B[X + 2, rows, :]
 
-        def relay_source(step):
-            return remote(GB.at[step], GB.at[step], gsend.at[step, 2], grecv.at[step],
-                          heart - 3, brick)
-
-        def wait_source(step):
-            remote(GB.at[step], GB.at[step], gsend.at[step, 2], grecv.at[step],
-                   heart, brick).wait_recv()
+        def relay_source(step, n):
+            return source_copy(step, n, 2, heart - 3)
+
+        def wait_source(step, n):
+            source_copy(step, n, 2, heart).wait_recv()
 
         def current_copy(step):
             inner = sec == heart - 3
@@ -379,20 +402,33 @@
                 return (center - 6.0) - T[x], store
             for_planes(0, X, 4, absorb)
 
-            def one_plane(x, carry):
-                SE[0, pl.ds(x, 1), :] = EB[x + 1, 0:1, :]
-                SE[1, pl.ds(x, 1), :] = EB[x + 1, pl.ds(Y - 1, 1), :]
-                return carry
-            lax.fori_loop(0, X, one_plane, 0, unroll=True)
+            for j, at in ((0, 0), (1, Y - 1)):
+                flat, where = across(EB, at, 1, X, Y)
+                SE[j] = flat[where, :]
             for there, src, dst, land, far, near, s, b in init_copies():
                 @pl.when(there)
                 def _():
                     remote(src, dst, isend.at[near], irecv.at[far], s, b).start()
 
+        BESIDE, ACROSS = (0, 1, 4, 5, 6, 7), (2, 3)
+
+        def second_sweep(slot, weight, scale, more):
+            wait_all(slot, True)
+            after = 1 - slot
+            work = plane(B, A, False, weight, scale)
+            done = [work(x) for x in (0, 1, X - 2, X - 1)]
+            for value, store in done:
+                store(value)
+            for low in (0, X - 2):
+                mend(A, low, low + 2, R2, 0, scale)
+            pack_corners()
+            send(after, BESIDE, more)
+            for_planes(2, X - 4, 7, work)
+            mend(A, 2, X - 2, R2, 0, scale)
+            pack_rows()
+            send(after, ACROSS, more)
+
         def step_body(step, carry):
-            pack()
-            send_all(0)
-
             @pl.when(step == 0)
             def _():
                 set_up()
@@ -425,14 +461,6 @@
             def _():
                 current_copy(step).start()
 
-            @pl.when(jnp.logical_or(sec != heart - 2, step == 0))
-            def _():
-                wait_source(step)
-
-            @pl.when(jnp.logical_and(sec == heart - 2, step == 0))
-            def _():
-                relay_source(step).start()
-
             flags = [jnp.where(PR[i] == section, 1.0, 0.0) for i in range(2)]
 
             def place(flag):
@@ -444,26 +472,29 @@
                         B[x + 2, rows, :] = B[x + 2, rows, :] + 0.5 * value
                     return value, store
                 return work
-            for_planes(0, X, 4, place(own))
-            for x, flag in ((-1, flags[0]), (X, flags[1])):
-                value, store = place(flag)(x)
-                store(value)
-
-            def source_rows(x, carry):
-                BR[0, pl.ds(x, 1), :] = own_y[0][0:1] * GB[step, x + 1, pl.ds(Y - 1, 1), :]
-                BR[1, pl.ds(x, 1), :] = own_y[1][0:1] * GB[step, x + 1, pl.ds(0, 1), :]
-                return carry
-            lax.fori_loop(0, X, source_rows, 0, unroll=True)
-            for j in range(2):
+            for n, (low, count) in enumerate(parts):
+                @pl.when(jnp.logical_or(sec != heart - 2, step == 0))
+                def _():
+                    wait_source(step, n)
+
+                @pl.when(jnp.logical_and(sec == heart - 2, step == 0))
+                def _():
+                    relay_source(step, n).start()
+                if n in inner:
+                    for_planes(low - 1, count, 5, place(own))
+                else:
+                    for x in (low - 1, low):
+                        value, store = place({-1: flags[0], X: flags[1]}.get(x, own))(x)
+                        store(value)
+
+            for j, at in ((0, Y - 1), (1, 0)):
+                flat, where = across(GB, at, step * (X + 2) + 1, X, Y)
+                BR[j] = jnp.broadcast_to(own_y[j][0:1], (X, Z)) * flat[where, :]
                 R2[j] = R2[j] + 0.5 * BR[j]
-            wait_all(0, True)
-            for_planes(0, X, 8, plane(B, A, False, push[1]))
-            mend(A, 0, X, R2, 0, 1.0)
+            second_sweep(0, push[1], 1.0, True)
 
             def group(g, carry):
                 slot = lax.rem(g, 2)
-                pack()
-                send_all(slot)
 
                 @pl.when(jnp.logical_and(g == 1, sec == heart - 2))
                 def _():
@@ -480,8 +511,9 @@
                 @pl.when(jnp.logical_and(jnp.logical_and(g == GROUPS - 3, step + 1 < STEPS),
                                          sec == heart - 2))
                 def _():
-                    wait_source(step + 1)
-                    relay_source(step + 1).start()
+                    for n in range(len(parts)):
+                        wait_source(step + 1, n)
+                        relay_source(step + 1, n).start()
 
                 first = push[2 * g]
                 for_planes(1, X - 2, 6, plane(A, B, False, first))
@@ -491,20 +523,17 @@
                 fringe(slot, False, first)
                 mend(B, -1, X + 1, R, PAD, 1.0)
                 close_edges()
-                wait_all(slot, True)
-                for_planes(0, X, 8, plane(B, A, False, push[2 * g + 1]))
-                mend(A, 0, X, R2, 0, 1.0)
+                second_sweep(slot, push[2 * g + 1], push[SWEEPS + g],
+                             jnp.logical_or(g < GROUPS - 1, step < STEPS - 1))
                 return carry
 
             lax.fori_loop(1, GROUPS, group, 0)
-
-            def scale(x):
-                def store(value):
-                    A[x + 2, rows, :] = value
-                return FINAL * A[x + 2, rows, :], store
-            for_planes(0, X, 8, scale)
             return carry
 
+        pack_corners()
+        send(0, BESIDE, True)
+        pack_rows()
+        send(0, ACROSS, True)
         lax.fori_loop(0, STEPS, step_body, 0)
 
         def write(x):
@@ -517,7 +546,8 @@
 
             @pl.when(sec == heart - 2)
             def _():
-                relay_source(step).wait_send()
+                for n in range(len(parts)):
+                    relay_source(step, n).wait_send()
 
     pl.when(is_heart)(heart_program)
     pl.when(jnp.logical_not(is_heart))(torso_program)
@@ -526,7 +556,6 @@
 def body(mesh, potentials, coefficient, recovery, excitable, row_of):
     sections, bricks = mesh.shape["sec"], mesh.shape["brick"]
     _, X, Y, Z = potentials.shape
-    row = jnp.broadcast_to(row_of.astype(jnp.float32)[:, None], (8, Z))
     f32 = jnp.float32
     scratch = [
         ((X + 4, Y + 2 * PAD, Z), f32), ((X + 4, Y + 2 * PAD, Z), f32),
@@ -537,25 +566,26 @@
         ((2, 2, X, Z), f32), ((4, 8, Z), f32),
         ((2, X + 2 * PAD, Z), f32), ((2, X, Z), f32),
         ((2, X, Z), f32), ((2, X, Z), f32), ((2, X, Z), f32),
-        ((2, 8, Z), f32), ((STEPS + 1, 2, 2, Y, Z), f32),
+        ((2, 8, Z), f32), ((STEPS + 1, 2, 2, Y, Z), f32), ((8, Z), f32),
     ]
-    sems = [(4,), (8,), (2, 8), (6,), (6,), (STEPS, 3), (STEPS,), (STEPS,), (STEPS, 2),
+    sems = [(4,), (8,), (2, 8), (6,), (6,), (STEPS, 5, 3), (STEPS, 5), (STEPS,), (STEPS, 2),
             (2,), (STEPS + 1, 2)]
     vmem = pl.BlockSpec(memory_space=pltpu.VMEM)
-    anywhere = pl.BlockSpec(memory_space=pl.ANY)
+    hbm = pl.BlockSpec(memory_space=pltpu.HBM)
     cells = X * Y * Z
     return pl.pallas_call(
         functools.partial(kernel, sections, bricks),
         out_shape=jax.ShapeDtypeStruct(potentials.shape, f32),
-        in_specs=[anywhere] * 4 + [pl.BlockSpec(memory_space=pltpu.SMEM), vmem],
+        in_specs=[hbm] * 4 + [pl.BlockSpec(memory_space=pltpu.SMEM)],
         out_specs=vmem,
         scratch_shapes=[pltpu.VMEM(s, t) for s, t in scratch]
+        + [pltpu.SMEM((len(PUSHES),), f32)]
         + [pltpu.SemaphoreType.DMA(s) for s in sems],
         compiler_params=pltpu.CompilerParams(
-            collective_id=0, has_side_effects=True, vmem_limit_bytes=40 * 2**20),
+            collective_id=0, has_side_effects=True, vmem_limit_bytes=63 * 2**20 + 2**19),
         cost_estimate=pl.CostEstimate(
             flops=cells * STEPS * SWEEPS * 12, bytes_accessed=20 * cells, transcendentals=0),
-    )(potentials, coefficient, recovery, excitable, jnp.asarray(np.array(PUSHES, np.float32)), row)
+    )(potentials, coefficient, recovery, excitable, row_of)
 
 
 def solution(mesh):

time: 94.6 us -> 80.1 us (0.85)
  Pallas kernels: 87.4 us -> 77.4 us
  local copies, waits for them, and re-layouts: 5.6 us -> 1.87 us
    pallas_call x1, Pallas kernels: 87.4 us -> 77.4 us  [body(): pl.pallas_call(functools.partial(kernel, sections, bricks), out_shape=jax...]
    unnamed x11 -> x1, local copies, waits for them, and re-layouts: 5.6 us -> 1.87 us
where the time goes in v2:
time: 80.1 us; the launch traced here: 80 us
  Pallas kernels  77.4 us (97%)
  local copies, waits for them, and re-layouts  1.87 us (2%)
    pallas_call x1, Pallas kernels, body(): pl.pallas_call(functools.partial(kernel, sections, bricks), out_shape=jax...  77.4 us
    unnamed x1, local copies, waits for them, and re-layouts  1.87 us

profile of v2, /device:TPU:0, one launch (start us, length us, event | category | flops | bytes accessed | tf_op | source)
XLA Modules:
  0.0 80.0 jit_solution(2162199030327636644)
XLA Ops:
  0.7 77.4 %shard_map.55 = f32[1,32,32,128]{3,2,1,0:T(8,128)} custom-call(f32[1,32,32,128]{3,2,1,0:T(8,128)} %pot.1, f32[1,32,32,128]{3,2,1,0:T(8,128)} %coef.1, f32[32,32,128]{2,1,0:T(8,128)} %rec.1, s32[32,32,128]{2,1,0:T(8,128)} %exc.1, s32[1]{0:T(128)S(6)} %copy.7.row_of), custom_call_target="tpu_custom_call" | custom-call | flops 50331648 | bytes 2621440 | tf_op jit(solution)/shard_map/pallas_call | solution.py:576
  78.1 1.9 %copy.8 = f32[1,32,32,128]{3,2,1,0:T(8,128)} copy(f32[1,32,32,128]{3,2,1,0:T(8,128)} %shard_map.55) | data formatting | bytes 1048576

commit v3 on v2

--- a/solution.py
+++ b/solution.py
@@ -57,8 +57,8 @@
 
 
 def kernel(sections, bricks, pot, coef, rec, exc, row_of, out,
-           A, B, EB, GB, BB, JA, JB, W, T, M, HX, HY, HC, SY, SC, R, R2, ER, SE, BR, PR, VH, row, push,
-           lsem, xsend, xrecv, isend, irecv, gsend, grecv, jsend, jrecv, vsend, vrecv):
+           A, B, EB, GB, BB, JA, JB, W, T, M, H, S, DUMP, ZB, R, R2, ER, SE, BR, PR, VH, row, push,
+           lsem, sent, landing, isend, irecv, gsend, grecv, jsend, jrecv, vsend, vrecv):
     X, Y, Z = W.shape
     sec = lax.axis_index("sec")
     brick = lax.axis_index("brick")
@@ -98,7 +98,7 @@
             return carry
 
         lax.fori_loop(0, X + 4, clear, 0)
-        for buf in (HX, HY, HC, ER, R2):
+        for buf in (ZB, ER, R2):
             buf[...] = jnp.zeros(buf.shape, jnp.float32)
         EB[0] = jnp.zeros((Y, Z), jnp.float32)
         EB[X + 1] = jnp.zeros((Y, Z), jnp.float32)
@@ -271,45 +271,73 @@
         own_y = (jnp.where(row[...] == section - 1.0, 1.0, 0.0),
                  jnp.where(row[...] == section + 1.0, 1.0, 0.0))
 
-        def messages(slot):
-            found = []
+        at_x = [(2 * Y * i, 2 * Y) for i in range(2)]
+        at_y = [(4 * Y + 2 * X * j, 2 * X) for j in range(2)]
+        at_c = [(4 * (X + Y) + 8 * n, 8) for n in range(4)]
+
+        def message(slot, there, here, s, b):
+            there_at, here_at = pl.ds(*there), pl.ds(*here)
+            return remote(S.at[slot, here_at], H.at[slot, there_at], sent.at[slot],
+                          landing.at[slot], s, b)
+
+        def nothing(slot, here):
+            zeros = ZB.at[pl.ds(0, here[1])]
+            pltpu.make_async_copy(zeros, H.at[slot, pl.ds(*here)], landing.at[slot]).start()
+            pltpu.make_async_copy(zeros, DUMP.at[slot, pl.ds(*here)], sent.at[slot]).start()
+
+        def send_beside(slot):
             for i in range(2):
-                found.append((has_x[i], A.at[pl.ds(2, 2) if i == 0 else pl.ds(X, 2), rows],
-                              HX.at[slot, 1 - i], HX.at[slot, i], 1 - i, i, sec, to_x[i]))
+                @pl.when(has_x[i])
+                def _():
+                    message(slot, at_x[1 - i], at_x[i], sec, to_x[i]).start()
+                    for j in range(2):
+                        n = 2 * i + j
+
+                        @pl.when(has_y[j])
+                        def _():
+                            message(slot, at_c[3 - n], at_c[n], to_y[j], to_x[i]).start()
+
+                        @pl.when(jnp.logical_not(has_y[j]))
+                        def _():
+                            nothing(slot, at_c[n])
+
+                @pl.when(jnp.logical_not(has_x[i]))
+                def _():
+                    nothing(slot, at_x[i])
+                    for j in range(2):
+                        nothing(slot, at_c[2 * i + j])
+
+        def send_across(slot):
             for j in range(2):
-                found.append((has_y[j], SY.at[j], HY.at[slot, 1 - j], HY.at[slot, j],
-                              3 - j, 2 + j, to_y[j], brick))
-            for n, (i, j) in enumerate(DIAGONAL):
-                found.append((jnp.logical_and(has_x[i], has_y[j]), SC.at[n], HC.at[slot, 3 - n],
-                              HC.at[slot, n], 7 - n, 4 + n, to_y[j], to_x[i]))
-            return found
-
-        def send(slot, which, more):
-            for there, src, dst, land, far, near, s, b in [messages(slot)[n] for n in which]:
-                @pl.when(jnp.logical_and(there, more))
-                def _():
-                    remote(src, dst, xsend.at[near], xrecv.at[slot, far], s, b).start()
-
-        def wait_all(slot, sent):
-            for there, src, dst, land, far, near, s, b in messages(slot):
-                @pl.when(there)
-                def _():
-                    got = remote(src, land, xsend.at[near], xrecv.at[slot, near], s, b)
-                    if sent:
-                        got.wait_send()
-                    else:
-                        got.wait_recv()
-
-        def pack_rows():
+                @pl.when(has_y[j])
+                def _():
+                    message(slot, at_y[1 - j], at_y[j], to_y[j], brick).start()
+
+                @pl.when(jnp.logical_not(has_y[j]))
+                def _():
+                    nothing(slot, at_y[j])
+
+        def wait_landed(slot):
+            pltpu.make_async_copy(S.at[slot], H.at[slot], landing.at[slot]).wait()
+
+        def wait_sent(slot):
+            pltpu.make_async_copy(S.at[slot], DUMP.at[slot], sent.at[slot]).wait()
+
+        def pack_rows(slot):
             for j in range(2):
                 for n in range(2):
                     at = PAD + n if j == 0 else PAD + Y - 1 - n
                     flat, where = across(A, at, 2, X, Y + 2 * PAD)
-                    SY[j, n] = flat[where, :]
-
-        def pack_corners():
+                    S[slot, pl.ds(at_y[j][0] + n * X, X), :] = flat[where, :]
+
+        def pack_planes(slot):
+            for i in range(2):
+                for n in range(2):
+                    value = A[(2 if i == 0 else X) + n, rows, :]
+                    S[slot, pl.ds(at_x[i][0] + n * Y, Y), :] = value
             for n, (i, j) in enumerate(DIAGONAL):
-                SC[n, 0:1, :] = A[2 if i == 0 else X + 1, pl.ds(PAD if j == 0 else PAD + Y - 1, 1), :]
+                corner = A[2 if i == 0 else X + 1, pl.ds(PAD if j == 0 else PAD + Y - 1, 1), :]
+                S[slot, pl.ds(at_c[n][0], 1), :] = corner
 
         def stencil(src, x):
             c = src[x + 2, rows, :]
@@ -343,7 +371,7 @@
             for j in range(2):
                 c = R[j, pl.ds(PAD, X), :]
                 total = R[j, pl.ds(PAD - 1, X), :] + R[j, pl.ds(PAD + 1, X), :]
-                total = total + SY[j, 0] + HY[slot, j, 1]
+                total = total + S[slot, pl.ds(at_y[j][0], X), :] + H[slot, pl.ds(at_y[j][0] + X, X), :]
                 total = total + jnp.where(lane_x == 0, 0.0, pltpu.roll(c, 1, 1))
                 total = total + jnp.where(lane_x == Z - 1, 0.0, pltpu.roll(c, Z - 1, 1))
                 total = total + ER[j] * c
@@ -354,20 +382,27 @@
 
         def landed(slot):
             for j in range(2):
-                A[j, rows, :] = HX[slot, 0, j]
-                A[X + 2 + j, rows, :] = HX[slot, 1, j]
-                R[j, pl.ds(PAD, X), :] = HY[slot, j, 0]
+                A[j, rows, :] = H[slot, pl.ds(at_x[0][0] + j * Y, Y), :]
+                A[X + 2 + j, rows, :] = H[slot, pl.ds(at_x[1][0] + j * Y, Y), :]
+                R[j, pl.ds(PAD, X), :] = H[slot, pl.ds(at_y[j][0], X), :]
             for n, (i, j) in enumerate(DIAGONAL):
-                R[j, pl.ds(PAD - 1 if i == 0 else PAD + X, 1), :] = HC[slot, n, 0:1, :]
-
-        def edges(first, weight):
-            for x in (-1, 0, X - 1, X):
-                value, store = plane(A, B, first, weight)(x)
+                R[j, pl.ds(PAD - 1 if i == 0 else PAD + X, 1), :] = H[slot, pl.ds(at_c[n][0], 1), :]
+
+        def first_sweep(slot, number, first, weight, prepare=lambda: None):
+            for_planes(1, X - 2, 6, plane(A, B, first, weight))
+
+            @pl.when(number > 0)
+            def _():
+                wait_sent(1 - slot)
+            wait_landed(slot)
+            prepare()
+            landed(slot)
+            done = [plane(A, B, first, weight, scale)(x) for x, scale in
+                    ((-1, inside_x[0]), (0, None), (X - 1, None), (X, inside_x[1]))]
+            for value, store in done:
                 store(value)
-
-        def close_edges():
-            B[1, rows, :] = inside_x[0] * B[1, rows, :]
-            B[X + 2, rows, :] = inside_x[1] * B[X + 2, rows, :]
+            fringe(slot, first, weight)
+            mend(B, -1, X + 1, R, PAD, 0.5 if first else 1.0)
 
         def relay_source(step, n):
             return source_copy(step, n, 2, heart - 3)
@@ -410,44 +445,43 @@
                 def _():
                     remote(src, dst, isend.at[near], irecv.at[far], s, b).start()
 
-        BESIDE, ACROSS = (0, 1, 4, 5, 6, 7), (2, 3)
-
         def second_sweep(slot, weight, scale, more):
-            wait_all(slot, True)
             after = 1 - slot
+            for j, at in ((0, PAD - 1), (1, PAD + Y)):
+                flat, where = across(B, at, 2, X, Y + 2 * PAD)
+                flat[where, :] = R2[j]
             work = plane(B, A, False, weight, scale)
             done = [work(x) for x in (0, 1, X - 2, X - 1)]
             for value, store in done:
                 store(value)
-            for low in (0, X - 2):
-                mend(A, low, low + 2, R2, 0, scale)
-            pack_corners()
-            send(after, BESIDE, more)
+
+            @pl.when(more)
+            def _():
+                pack_planes(after)
+                send_beside(after)
             for_planes(2, X - 4, 7, work)
-            mend(A, 2, X - 2, R2, 0, scale)
-            pack_rows()
-            send(after, ACROSS, more)
+
+            @pl.when(more)
+            def _():
+                pack_rows(after)
+                send_across(after)
 
         def step_body(step, carry):
             @pl.when(step == 0)
             def _():
                 set_up()
-            for_planes(1, X - 2, 6, plane(A, B, True, None))
-            wait_all(0, False)
-
-            @pl.when(step == 0)
-            def _():
-                for there, src, dst, land, far, near, s, b in init_copies():
-                    @pl.when(there)
-                    def _():
-                        got = remote(src, land, isend.at[near], irecv.at[near], s, b)
-                        got.wait_recv()
-                        got.wait_send()
-            landed(0)
-            edges(True, None)
-            fringe(0, True, None)
-            mend(B, -1, X + 1, R, PAD, 0.5)
-            close_edges()
+
+            def prepare():
+                @pl.when(step == 0)
+                def _():
+                    for there, src, dst, land, far, near, s, b in init_copies():
+                        @pl.when(there)
+                        def _():
+                            got = remote(src, land, isend.at[near], irecv.at[near], s, b)
+                            got.wait_recv()
+                            got.wait_send()
+
+            first_sweep(0, step, True, None, prepare)
 
             def current(x):
                 def store(value):
@@ -491,7 +525,7 @@
                 flat, where = across(GB, at, step * (X + 2) + 1, X, Y)
                 BR[j] = jnp.broadcast_to(own_y[j][0:1], (X, Z)) * flat[where, :]
                 R2[j] = R2[j] + 0.5 * BR[j]
-            second_sweep(0, push[1], 1.0, True)
+            second_sweep(0, push[1], None, True)
 
             def group(g, carry):
                 slot = lax.rem(g, 2)
@@ -516,13 +550,7 @@
                         relay_source(step + 1, n).start()
 
                 first = push[2 * g]
-                for_planes(1, X - 2, 6, plane(A, B, False, first))
-                wait_all(slot, False)
-                landed(slot)
-                edges(False, first)
-                fringe(slot, False, first)
-                mend(B, -1, X + 1, R, PAD, 1.0)
-                close_edges()
+                first_sweep(slot, g, False, first)
                 second_sweep(slot, push[2 * g + 1], push[SWEEPS + g],
                              jnp.logical_or(g < GROUPS - 1, step < STEPS - 1))
                 return carry
@@ -530,10 +558,10 @@
             lax.fori_loop(1, GROUPS, group, 0)
             return carry
 
-        pack_corners()
-        send(0, BESIDE, True)
-        pack_rows()
-        send(0, ACROSS, True)
+        pack_planes(0)
+        send_beside(0)
+        pack_rows(0)
+        send_across(0)
         lax.fori_loop(0, STEPS, step_body, 0)
 
         def write(x):
@@ -541,6 +569,7 @@
                 out[0, x] = value
             return A[x + 2, rows, :], store
         for_planes(0, X, 8, write)
+        wait_sent((GROUPS - 1) % 2)
         for step in range(STEPS):
             current_copy(step).wait_send()
 
@@ -562,13 +591,13 @@
         ((X + 2, Y, Z), f32), ((STEPS, X + 2, Y, Z), f32), ((X + 2, Y, Z), f32),
         ((STEPS, X, Y, Z), f32), ((STEPS, 2, X, Y, Z), f32),
         ((X, Y, Z), f32), ((X, Y, Z), f32), ((X, Y, Z), jnp.int32),
-        ((2, 2, 2, Y, Z), f32), ((2, 2, 2, X, Z), f32), ((2, 4, 8, Z), f32),
-        ((2, 2, X, Z), f32), ((4, 8, Z), f32),
+        ((2, 4 * (X + Y) + 32, Z), f32), ((2, 4 * (X + Y) + 32, Z), f32),
+        ((2, 4 * (X + Y) + 32, Z), f32), ((2 * max(X, Y), Z), f32),
         ((2, X + 2 * PAD, Z), f32), ((2, X, Z), f32),
         ((2, X, Z), f32), ((2, X, Z), f32), ((2, X, Z), f32),
         ((2, 8, Z), f32), ((STEPS + 1, 2, 2, Y, Z), f32), ((8, Z), f32),
     ]
-    sems = [(4,), (8,), (2, 8), (6,), (6,), (STEPS, 5, 3), (STEPS, 5), (STEPS,), (STEPS, 2),
+    sems = [(4,), (2,), (2,), (6,), (6,), (STEPS, 5, 3), (STEPS, 5), (STEPS,), (STEPS, 2),
             (2,), (STEPS + 1, 2)]
     vmem = pl.BlockSpec(memory_space=pltpu.VMEM)
     hbm = pl.BlockSpec(memory_space=pltpu.HBM)

time: 80.1 us -> 79.3 us (0.990)
    pallas_call x1, Pallas kernels: 77.4 us -> 76.6 us  [body(): pl.pallas_call(functools.partial(kernel, sections, bricks), out_shape=jax...]
where the time goes in v3:
time: 79.3 us; the launch traced here: 79.1 us
  Pallas kernels  76.6 us (97%)
  local copies, waits for them, and re-layouts  1.87 us (2%)
    pallas_call x1, Pallas kernels, body(): pl.pallas_call(functools.partial(kernel, sections, bricks), out_shape=jax...  76.6 us
    unnamed x1, local copies, waits for them, and re-layouts  1.87 us

profile of v3, /device:TPU:0, one launch (start us, length us, event | category | flops | bytes accessed | tf_op | source)
XLA Modules:
  0.0 79.1 jit_solution(17573713737856090381)
XLA Ops:
  0.7 76.6 %shard_map.55 = f32[1,32,32,128]{3,2,1,0:T(8,128)} custom-call(f32[1,32,32,128]{3,2,1,0:T(8,128)} %pot.1, f32[1,32,32,128]{3,2,1,0:T(8,128)} %coef.1, f32[32,32,128]{2,1,0:T(8,128)} %rec.1, s32[32,32,128]{2,1,0:T(8,128)} %exc.1, s32[1]{0:T(128)S(6)} %copy.7.row_of), custom_call_target="tpu_custom_call" | custom-call | flops 50331648 | bytes 2621440 | tf_op jit(solution)/shard_map/pallas_call | solution.py:605
  77.2 1.9 %copy.8 = f32[1,32,32,128]{3,2,1,0:T(8,128)} copy(f32[1,32,32,128]{3,2,1,0:T(8,128)} %shard_map.55) | data formatting | bytes 1048576

commit v4 on v3

--- a/solution.py
+++ b/solution.py
@@ -253,9 +253,12 @@
 
                 def final(x):
                     def store(value):
-                        out[0, x] = value
+                        BB[x] = value
                     return BB[x] + coupling_gain * (JB[step, 0, x] + JB[step, 1, x]), store
                 for_planes(0, X, 4, final)
+                result = pltpu.make_async_copy(BB.at[pl.ds(0, X)], out.at[0], lsem.at[0])
+                result.start()
+                result.wait()
         for step in range(STEPS):
             for n in range(len(parts)):
                 for far in (2, 1):
@@ -286,26 +289,37 @@
             pltpu.make_async_copy(zeros, DUMP.at[slot, pl.ds(*here)], sent.at[slot]).start()
 
         def send_beside(slot):
-            for i in range(2):
+            for n, (i, j) in enumerate(DIAGONAL):
+                both = jnp.logical_and(has_x[i], has_y[j])
+
+                @pl.when(both)
+                def _():
+                    message(slot, at_c[3 - n], at_c[n], to_y[j], to_x[i]).start()
+
+                @pl.when(jnp.logical_not(both))
+                def _():
+                    nothing(slot, at_c[n])
+
+            def send_planes(i):
                 @pl.when(has_x[i])
                 def _():
                     message(slot, at_x[1 - i], at_x[i], sec, to_x[i]).start()
-                    for j in range(2):
-                        n = 2 * i + j
-
-                        @pl.when(has_y[j])
-                        def _():
-                            message(slot, at_c[3 - n], at_c[n], to_y[j], to_x[i]).start()
-
-                        @pl.when(jnp.logical_not(has_y[j]))
-                        def _():
-                            nothing(slot, at_c[n])
 
                 @pl.when(jnp.logical_not(has_x[i]))
                 def _():
                     nothing(slot, at_x[i])
-                    for j in range(2):
-                        nothing(slot, at_c[2 * i + j])
+
+            even = lax.rem(brick, 2) == 0
+
+            @pl.when(even)
+            def _():
+                send_planes(0)
+                send_planes(1)
+
+            @pl.when(jnp.logical_not(even))
+            def _():
+                send_planes(1)
+                send_planes(0)
 
         def send_across(slot):
             for j in range(2):
@@ -551,8 +565,9 @@
 
                 first = push[2 * g]
                 first_sweep(slot, g, False, first)
-                second_sweep(slot, push[2 * g + 1], push[SWEEPS + g],
-                             jnp.logical_or(g < GROUPS - 1, step < STEPS - 1))
+                going_on = step < STEPS - 1
+                second_sweep(slot, push[2 * g + 1], jnp.where(going_on, push[SWEEPS + g], 1.0),
+                             jnp.logical_or(g < GROUPS - 1, going_on))
                 return carry
 
             lax.fori_loop(1, GROUPS, group, 0)
@@ -564,11 +579,8 @@
         send_across(0)
         lax.fori_loop(0, STEPS, step_body, 0)
 
-        def write(x):
-            def store(value):
-                out[0, x] = value
-            return A[x + 2, rows, :], store
-        for_planes(0, X, 8, write)
+        result = pltpu.make_async_copy(A.at[pl.ds(2, X), rows], out.at[0], lsem.at[0])
+        result.start()
         wait_sent((GROUPS - 1) % 2)
         for step in range(STEPS):
             current_copy(step).wait_send()
@@ -577,6 +589,8 @@
             def _():
                 for n in range(len(parts)):
                     relay_source(step, n).wait_send()
+
+        result.wait()
 
     pl.when(is_heart)(heart_program)
     pl.when(jnp.logical_not(is_heart))(torso_program)
@@ -599,14 +613,13 @@
     ]
     sems = [(4,), (2,), (2,), (6,), (6,), (STEPS, 5, 3), (STEPS, 5), (STEPS,), (STEPS, 2),
             (2,), (STEPS + 1, 2)]
-    vmem = pl.BlockSpec(memory_space=pltpu.VMEM)
     hbm = pl.BlockSpec(memory_space=pltpu.HBM)
     cells = X * Y * Z
-    return pl.pallas_call(
+    fields = pl.pallas_call(
         functools.partial(kernel, sections, bricks),
         out_shape=jax.ShapeDtypeStruct(potentials.shape, f32),
         in_specs=[hbm] * 4 + [pl.BlockSpec(memory_space=pltpu.SMEM)],
-        out_specs=vmem,
+        out_specs=hbm,
         scratch_shapes=[pltpu.VMEM(s, t) for s, t in scratch]
         + [pltpu.SMEM((len(PUSHES),), f32)]
         + [pltpu.SemaphoreType.DMA(s) for s in sems],
@@ -615,6 +628,8 @@
         cost_estimate=pl.CostEstimate(
             flops=cells * STEPS * SWEEPS * 12, bytes_accessed=20 * cells, transcendentals=0),
     )(potentials, coefficient, recovery, excitable, row_of)
+    torso = lax.axis_index("sec") < sections - 1
+    return fields * jnp.where(torso, PUSHES[-1], 1.0).astype(f32)
 
 
 def solution(mesh):

time: 79.3 us -> 77.9 us (0.982)
  other arithmetic: 0 us -> 1.88 us
  local copies, waits for them, and re-layouts: 1.87 us -> 0 us
  Pallas kernels: 76.6 us -> 75.2 us
    mul x0 -> x1, other arithmetic: none -> 1.88 us  [body(): return fields * jnp.where(torso, PUSHES[-1], 1.0).astype(f32)]
    unnamed x1 -> x0, local copies, waits for them, and re-layouts: 1.87 us -> none
    pallas_call x1, Pallas kernels: 76.6 us -> 75.2 us  [body(): pl.pallas_call(functools.partial(kernel, sections, bricks), out_shape=jax...]
where the time goes in v4:
time: 77.9 us; the launch traced here: 77.8 us
  Pallas kernels  75.2 us (97%)
  other arithmetic  1.88 us (2%)
    pallas_call x1, Pallas kernels, body(): pl.pallas_call(functools.partial(kernel, sections, bricks), out_shape=jax...  75.2 us
    mul x1, other arithmetic, body(): return fields * jnp.where(torso, PUSHES[-1], 1.0).astype(f32)  1.88 us

profile of v4, /device:TPU:0, one launch (start us, length us, event | category | flops | bytes accessed | tf_op | source)
XLA Modules:
  0.0 77.8 jit_solution(12892446452905834331)
XLA Ops:
  0.7 75.2 %shard_map.55 = f32[1,32,32,128]{3,2,1,0:T(8,128)} custom-call(f32[1,32,32,128]{3,2,1,0:T(8,128)} %pot.1, f32[1,32,32,128]{3,2,1,0:T(8,128)} %coef.1, f32[32,32,128]{2,1,0:T(8,128)} %rec.1, s32[32,32,128]{2,1,0:T(8,128)} %exc.1, s32[1]{0:T(128)S(6)} %copy.6.row_of), custom_call_target="tpu_custom_call" | custom-call | flops 50331648 | bytes 2621440 | tf_op jit(solution)/shard_map/pallas_call | solution.py:618
  75.9 1.9 %broadcast_multiply_fusion = f32[1,32,32,128]{3,2,1,0:T(8,128)} fusion(f32[1,32,32,128]{3,2,1,0:T(8,128)} %shard_map.55, f32[]{:T(128)S(6)} %select_n.4), kind=kLoop, calls=%fused_computation | loop fusion | flops 131072 | bytes 1048580 | tf_op jit(solution)/shard_map/mul | solution.py:632

commit v5 on v4

--- a/solution.py
+++ b/solution.py
@@ -54,6 +54,12 @@
         return carry
 
     lax.fori_loop(0, count // unroll, chunk, 0)
+
+
+def in_line(first, count, work):
+    for x in range(first, first + count):
+        value, store = work(x)
+        store(value)
 
 
 def kernel(sections, bricks, pot, coef, rec, exc, row_of, out,
@@ -403,7 +409,7 @@
                 R[j, pl.ds(PAD - 1 if i == 0 else PAD + X, 1), :] = H[slot, pl.ds(at_c[n][0], 1), :]
 
         def first_sweep(slot, number, first, weight, prepare=lambda: None):
-            for_planes(1, X - 2, 6, plane(A, B, first, weight))
+            in_line(1, X - 2, plane(A, B, first, weight))
 
             @pl.when(number > 0)
             def _():
@@ -473,7 +479,7 @@
             def _():
                 pack_planes(after)
                 send_beside(after)
-            for_planes(2, X - 4, 7, work)
+            in_line(2, X - 4, work)
 
             @pl.when(more)
             def _():

time: 77.9 us -> 76.8 us (0.986)
  Pallas kernels: 75.2 us -> 74.1 us
    pallas_call x1, Pallas kernels: 75.2 us -> 74.1 us  [body(): pl.pallas_call(functools.partial(kernel, sections, bricks), out_shape=jax...]
where the time goes in v5:
time: 76.8 us; the launch traced here: 76.7 us
  Pallas kernels  74.1 us (96%)
  other arithmetic  1.88 us (2%)
    pallas_call x1, Pallas kernels, body(): pl.pallas_call(functools.partial(kernel, sections, bricks), out_shape=jax...  74.1 us
    mul x1, other arithmetic, body(): return fields * jnp.where(torso, PUSHES[-1], 1.0).astype(f32)  1.88 us

profile of v5, /device:TPU:0, one launch (start us, length us, event | category | flops | bytes accessed | tf_op | source)
XLA Modules:
  0.0 76.7 jit_solution(1629075741395292983)
XLA Ops:
  0.7 74.1 %shard_map.55 = f32[1,32,32,128]{3,2,1,0:T(8,128)} custom-call(f32[1,32,32,128]{3,2,1,0:T(8,128)} %pot.1, f32[1,32,32,128]{3,2,1,0:T(8,128)} %coef.1, f32[32,32,128]{2,1,0:T(8,128)} %rec.1, s32[32,32,128]{2,1,0:T(8,128)} %exc.1, s32[1]{0:T(128)S(6)} %copy.6.row_of), custom_call_target="tpu_custom_call" | custom-call | flops 50331648 | bytes 2621440 | tf_op jit(solution)/shard_map/pallas_call | solution.py:624
  74.8 1.9 %broadcast_multiply_fusion = f32[1,32,32,128]{3,2,1,0:T(8,128)} fusion(f32[1,32,32,128]{3,2,1,0:T(8,128)} %shard_map.55, f32[]{:T(128)S(6)} %select_n.4), kind=kLoop, calls=%fused_computation | loop fusion | flops 131072 | bytes 1048580 | tf_op jit(solution)/shard_map/mul | solution.py:638

commit v6 on v5

--- a/solution.py
+++ b/solution.py
@@ -294,7 +294,7 @@
             pltpu.make_async_copy(zeros, H.at[slot, pl.ds(*here)], landing.at[slot]).start()
             pltpu.make_async_copy(zeros, DUMP.at[slot, pl.ds(*here)], sent.at[slot]).start()
 
-        def send_beside(slot):
+        def send_corners(slot):
             for n, (i, j) in enumerate(DIAGONAL):
                 both = jnp.logical_and(has_x[i], has_y[j])
 
@@ -306,26 +306,18 @@
                 def _():
                     nothing(slot, at_c[n])
 
-            def send_planes(i):
-                @pl.when(has_x[i])
+        def send_planes(slot, longer):
+            even = lax.rem(brick, 2) == 0
+            for i in range(2):
+                mine = even if (i == 0) == longer else jnp.logical_not(even)
+
+                @pl.when(jnp.logical_and(mine, has_x[i]))
                 def _():
                     message(slot, at_x[1 - i], at_x[i], sec, to_x[i]).start()
 
-                @pl.when(jnp.logical_not(has_x[i]))
+                @pl.when(jnp.logical_and(mine, jnp.logical_not(has_x[i])))
                 def _():
                     nothing(slot, at_x[i])
-
-            even = lax.rem(brick, 2) == 0
-
-            @pl.when(even)
-            def _():
-                send_planes(0)
-                send_planes(1)
-
-            @pl.when(jnp.logical_not(even))
-            def _():
-                send_planes(1)
-                send_planes(0)
 
         def send_across(slot):
             for j in range(2):
@@ -478,8 +470,15 @@
             @pl.when(more)
             def _():
                 pack_planes(after)
-                send_beside(after)
-            in_line(2, X - 4, work)
+                send_corners(after)
+                send_planes(after, True)
+            half = (X - 4) // 2
+            in_line(2, half, work)
+
+            @pl.when(more)
+            def _():
+                send_planes(after, False)
+            in_line(2 + half, X - 4 - half, work)
 
             @pl.when(more)
             def _():
@@ -580,7 +579,9 @@
             return carry
 
         pack_planes(0)
-        send_beside(0)
+        send_corners(0)
+        send_planes(0, True)
+        send_planes(0, False)
         pack_rows(0)
         send_across(0)
         lax.fori_loop(0, STEPS, step_body, 0)

time: 76.8 us -> 78.1 us (1.017)
  Pallas kernels: 74.1 us -> 75.4 us
    pallas_call x1, Pallas kernels: 74.1 us -> 75.4 us  [body(): pl.pallas_call(functools.partial(kernel, sections, bricks), out_shape=jax...]
where the time goes in v6:
time: 78.1 us; the launch traced here: 78 us
  Pallas kernels  75.4 us (97%)
  other arithmetic  1.88 us (2%)
    pallas_call x1, Pallas kernels, body(): pl.pallas_call(functools.partial(kernel, sections, bricks), out_shape=jax...  75.4 us
    mul x1, other arithmetic, body(): return fields * jnp.where(torso, PUSHES[-1], 1.0).astype(f32)  1.88 us

profile of v6, /device:TPU:0, one launch (start us, length us, event | category | flops | bytes accessed | tf_op | source)
XLA Modules:
  0.0 78.0 jit_solution(18286447890305238259)
XLA Ops:
  0.7 75.4 %shard_map.55 = f32[1,32,32,128]{3,2,1,0:T(8,128)} custom-call(f32[1,32,32,128]{3,2,1,0:T(8,128)} %pot.1, f32[1,32,32,128]{3,2,1,0:T(8,128)} %coef.1, f32[32,32,128]{2,1,0:T(8,128)} %rec.1, s32[32,32,128]{2,1,0:T(8,128)} %exc.1, s32[1]{0:T(128)S(6)} %copy.6.row_of), custom_call_target="tpu_custom_call" | custom-call | flops 50331648 | bytes 2621440 | tf_op jit(solution)/shard_map/pallas_call | solution.py:625
  76.1 1.9 %broadcast_multiply_fusion = f32[1,32,32,128]{3,2,1,0:T(8,128)} fusion(f32[1,32,32,128]{3,2,1,0:T(8,128)} %shard_map.55, f32[]{:T(128)S(6)} %select_n.4), kind=kLoop, calls=%fused_computation | loop fusion | flops 131072 | bytes 1048580 | tf_op jit(solution)/shard_map/mul | solution.py:639

commit v7 on v5

--- a/solution.py
+++ b/solution.py
@@ -359,26 +359,32 @@
                 corner = A[2 if i == 0 else X + 1, pl.ds(PAD if j == 0 else PAD + Y - 1, 1), :]
                 S[slot, pl.ds(at_c[n][0], 1), :] = corner
 
-        def stencil(src, x):
-            c = src[x + 2, rows, :]
-            total = src[x + 1, rows, :] + src[x + 3, rows, :]
-            total = total + (src[x + 2, pl.ds(PAD - 1, Y), :] + src[x + 2, pl.ds(PAD + 1, Y), :])
-            total = total + (jnp.where(lane == 0, 0.0, pltpu.roll(c, 1, 1))
-                             + jnp.where(lane == Z - 1, 0.0, pltpu.roll(c, Z - 1, 1)))
-            return total + EB[x + 1] * c
-
-        def plane(src, dst, first, weight, scale=None):
+        def stencil(src, x, low, high):
+            here = pl.ds(PAD + low, high - low)
+            at_lane = lane[0:high - low]
+            c = src[x + 2, here, :]
+            total = src[x + 1, here, :] + src[x + 3, here, :]
+            total = total + (src[x + 2, pl.ds(PAD + low - 1, high - low), :]
+                             + src[x + 2, pl.ds(PAD + low + 1, high - low), :])
+            total = total + (jnp.where(at_lane == 0, 0.0, pltpu.roll(c, 1, 1))
+                             + jnp.where(at_lane == Z - 1, 0.0, pltpu.roll(c, Z - 1, 1)))
+            return total + EB[x + 1, pl.ds(low, high - low), :] * c
+
+        def plane(src, dst, first, weight, scale=None, low=0, high=Y):
+            here = pl.ds(PAD + low, high - low)
+
             def work(x):
-                value = stencil(src, x)
+                value = stencil(src, x, low, high)
                 if first:
                     value = 0.5 * value
                 else:
-                    value = (value + weight * BB[x + 1]) - back * dst[x + 2, rows, :]
+                    value = ((value + weight * BB[x + 1, pl.ds(low, high - low), :])
+                             - back * dst[x + 2, here, :])
                 if scale is not None:
                     value = scale * value
 
                 def store(value):
-                    dst[x + 2, rows, :] = value
+                    dst[x + 2, here, :] = value
                 return value, store
             return work
 
@@ -430,12 +436,16 @@
         def wait_source(step, n):
             source_copy(step, n, 2, heart).wait_recv()
 
-        def current_copy(step):
-            inner = sec == heart - 3
-            target = jnp.where(inner, heart - 2, heart)
+        inner_layer = sec == heart - 3
+        pieces = largest_divisor(X, 4)
+        piece = X // pieces
+
+        def current_copy(step, low, count):
+            target = jnp.where(inner_layer, heart - 2, heart)
             place = jnp.where(sec == heart - 2, 1, 0)
-            return remote(JA.at[step], JB.at[step, place], jsend.at[step], jrecv.at[step, place],
-                          target, brick)
+            span = pl.ds(low, count)
+            return remote(JA.at[step, span], JB.at[step, place, span], jsend.at[step],
+                          jrecv.at[step, place], target, brick)
 
         def init_copies():
             found = []
@@ -479,12 +489,16 @@
             def _():
                 pack_planes(after)
                 send_beside(after)
-            in_line(2, X - 4, work)
+            band = 8 if Y > 16 else Y // 2
+            for low in (0, Y - band):
+                in_line(2, X - 4, plane(B, A, False, weight, scale, low, low + band))
 
             @pl.when(more)
             def _():
                 pack_rows(after)
                 send_across(after)
+            if Y > 2 * band:
+                in_line(2, X - 4, plane(B, A, False, weight, scale, band, Y - band))
 
         def step_body(step, carry):
             @pl.when(step == 0)
@@ -511,9 +525,9 @@
                 return own_v * value, store
             for_planes(0, X, 4, current)
 
-            @pl.when(sec != heart - 2)
-            def _():
-                current_copy(step).start()
+            @pl.when(inner_layer)
+            def _():
+                current_copy(step, 0, X).start()
 
             flags = [jnp.where(PR[i] == section, 1.0, 0.0) for i in range(2)]
 
@@ -560,7 +574,10 @@
                             JA[step, x] = value
                         return JA[step, x] + JB[step, 0, x], store
                     for_planes(0, X, 4, add)
-                    current_copy(step).start()
+
+                @pl.when(jnp.logical_and(g <= pieces, jnp.logical_not(inner_layer)))
+                def _():
+                    current_copy(step, (g - 1) * piece, piece).start()
 
                 @pl.when(jnp.logical_and(jnp.logical_and(g == GROUPS - 3, step + 1 < STEPS),
                                          sec == heart - 2))
@@ -589,7 +606,7 @@
         result.start()
         wait_sent((GROUPS - 1) % 2)
         for step in range(STEPS):
-            current_copy(step).wait_send()
+            current_copy(step, 0, X).wait_send()
 
             @pl.when(sec == heart - 2)
             def _():

time: 76.8 us -> 73.5 us (0.957)
  Pallas kernels: 74.1 us -> 70.8 us
    pallas_call x1, Pallas kernels: 74.1 us -> 70.8 us  [body(): pl.pallas_call(functools.partial(kernel, sections, bricks), out_shape=jax...]
where the time goes in v7:
time: 73.5 us; the launch traced here: 73.4 us
  Pallas kernels  70.8 us (96%)
  other arithmetic  1.88 us (3%)
    pallas_call x1, Pallas kernels, body(): pl.pallas_call(functools.partial(kernel, sections, bricks), out_shape=jax...  70.8 us
    mul x1, other arithmetic, body(): return fields * jnp.where(torso, PUSHES[-1], 1.0).astype(f32)  1.88 us

profile of v7, /device:TPU:0, one launch (start us, length us, event | category | flops | bytes accessed | tf_op | source)
XLA Modules:
  0.0 73.4 jit_solution(17283156847661558241)
XLA Ops:
  0.7 70.8 %shard_map.55 = f32[1,32,32,128]{3,2,1,0:T(8,128)} custom-call(f32[1,32,32,128]{3,2,1,0:T(8,128)} %pot.1, f32[1,32,32,128]{3,2,1,0:T(8,128)} %coef.1, f32[32,32,128]{2,1,0:T(8,128)} %rec.1, s32[32,32,128]{2,1,0:T(8,128)} %exc.1, s32[1]{0:T(128)S(6)} %copy.6.row_of), custom_call_target="tpu_custom_call" | custom-call | flops 50331648 | bytes 2621440 | tf_op jit(solution)/shard_map/pallas_call | solution.py:641
  71.5 1.9 %broadcast_multiply_fusion = f32[1,32,32,128]{3,2,1,0:T(8,128)} fusion(f32[1,32,32,128]{3,2,1,0:T(8,128)} %shard_map.55, f32[]{:T(128)S(6)} %select_n.4), kind=kLoop, calls=%fused_computation | loop fusion | flops 131072 | bytes 1048580 | tf_op jit(solution)/shard_map/mul | solution.py:655

commit v8 on v7

--- a/solution.py
+++ b/solution.py
@@ -129,8 +129,6 @@
             pl.semaphore_signal(barrier, inc=1, device_id={"sec": to_y[j], "brick": to_x[i]},
                                 device_id_type=MESH)
         total = total + both.astype(jnp.int32)
-    pl.semaphore_wait(barrier, total)
-    field.wait()
 
     cuts = largest_divisor(X - 2, 3)
     size = (X - 2) // cuts
@@ -141,11 +139,9 @@
         ref = GB.at[step, pl.ds(parts[n][0], parts[n][1])]
         return remote(ref, ref, gsend.at[step, n, lane_number], grecv.at[step, n], target, brick)
 
-    def heart_program():
+    def heart_program(early):
         recover = pltpu.make_async_copy(rec, W, lsem.at[2])
         excite = pltpu.make_async_copy(exc, M, lsem.at[3])
-        recover.start()
-        excite.start()
 
         def send_sides(round_number):
             for i in range(2):
@@ -210,7 +206,7 @@
                 W[x] = value[1]
             return (v, w), store
 
-        def source(step, chunks):
+        def sum_up(step, chunks):
             def work(x):
                 def store(value):
                     GB[step, x + 1] = value
@@ -218,6 +214,9 @@
             for n in chunks:
                 low, count = parts[n]
                 for_planes(low - 1, count, 5, work)
+
+        def hand_out(step, chunks):
+            for n in chunks:
                 for far in (2, 1):
                     source_copy(step, n, far - 1, heart - far).start()
 
@@ -226,11 +225,17 @@
                 remote(JB.at[step, n], JB.at[step, n], jsend.at[step], jrecv.at[step, n],
                        heart - 1 - n, brick).wait_recv()
 
-        edge_rows(2, X + 2)
+        if early:
+            recover.start()
+            excite.start()
+            edge_rows(2, X + 2)
+            sum_up(0, inner)
+            return
         send_sides(0)
-        source(0, inner)
+        hand_out(0, inner)
         sides(0)
-        source(0, outer)
+        sum_up(0, outer)
+        hand_out(0, outer)
         second.wait()
         recover.wait()
         excite.wait()
@@ -240,7 +245,8 @@
             edge_rows(2, X + 2)
             sides(step + 1)
             if step + 1 < STEPS:
-                source(step + 1, range(len(parts)))
+                sum_up(step + 1, range(len(parts)))
+                hand_out(step + 1, range(len(parts)))
                 current(step)
 
                 def advance(x):
@@ -270,7 +276,7 @@
                 for far in (2, 1):
                     source_copy(step, n, far - 1, heart - far).wait_send()
 
-    def torso_program():
+    def torso_program(early):
         one = jnp.ones((), jnp.float32)
         zero = jnp.zeros((), jnp.float32)
         inside_x = [jnp.where(h, one, zero) for h in has_x]
@@ -294,7 +300,7 @@
             pltpu.make_async_copy(zeros, H.at[slot, pl.ds(*here)], landing.at[slot]).start()
             pltpu.make_async_copy(zeros, DUMP.at[slot, pl.ds(*here)], sent.at[slot]).start()
 
-        def send_beside(slot):
+        def send_corners(slot):
             for n, (i, j) in enumerate(DIAGONAL):
                 both = jnp.logical_and(has_x[i], has_y[j])
 
@@ -306,7 +312,8 @@
                 def _():
                     nothing(slot, at_c[n])
 
-            def send_planes(i):
+        def send_planes(slot):
+            for i in range(2):
                 @pl.when(has_x[i])
                 def _():
                     message(slot, at_x[1 - i], at_x[i], sec, to_x[i]).start()
@@ -314,18 +321,6 @@
                 @pl.when(jnp.logical_not(has_x[i]))
                 def _():
                     nothing(slot, at_x[i])
-
-            even = lax.rem(brick, 2) == 0
-
-            @pl.when(even)
-            def _():
-                send_planes(0)
-                send_planes(1)
-
-            @pl.when(jnp.logical_not(even))
-            def _():
-                send_planes(1)
-                send_planes(0)
 
         def send_across(slot):
             for j in range(2):
@@ -355,6 +350,7 @@
                 for n in range(2):
                     value = A[(2 if i == 0 else X) + n, rows, :]
                     S[slot, pl.ds(at_x[i][0] + n * Y, Y), :] = value
+        def pack_corners(slot):
             for n, (i, j) in enumerate(DIAGONAL):
                 corner = A[2 if i == 0 else X + 1, pl.ds(PAD if j == 0 else PAD + Y - 1, 1), :]
                 S[slot, pl.ds(at_c[n][0], 1), :] = corner
@@ -470,41 +466,42 @@
             for j, at in ((0, 0), (1, Y - 1)):
                 flat, where = across(EB, at, 1, X, Y)
                 SE[j] = flat[where, :]
-            for there, src, dst, land, far, near, s, b in init_copies():
-                @pl.when(there)
-                def _():
-                    remote(src, dst, isend.at[near], irecv.at[far], s, b).start()
+            pack_rows(0)
+            pack_corners(0)
+            pack_planes(0)
+
+        if early:
+            set_up()
+            return
 
         def second_sweep(slot, weight, scale, more):
             after = 1 - slot
             for j, at in ((0, PAD - 1), (1, PAD + Y)):
                 flat, where = across(B, at, 2, X, Y + 2 * PAD)
                 flat[where, :] = R2[j]
-            work = plane(B, A, False, weight, scale)
-            done = [work(x) for x in (0, 1, X - 2, X - 1)]
-            for value, store in done:
-                store(value)
-
-            @pl.when(more)
-            def _():
-                pack_planes(after)
-                send_beside(after)
             band = 8 if Y > 16 else Y // 2
             for low in (0, Y - band):
-                in_line(2, X - 4, plane(B, A, False, weight, scale, low, low + band))
+                in_line(0, X, plane(B, A, False, weight, scale, low, low + band))
 
             @pl.when(more)
             def _():
                 pack_rows(after)
                 send_across(after)
+                pack_corners(after)
+                send_corners(after)
+            work = plane(B, A, False, weight, scale, band, Y - band)
             if Y > 2 * band:
-                in_line(2, X - 4, plane(B, A, False, weight, scale, band, Y - band))
+                for low in (0, X - 2):
+                    in_line(low, 2, work)
+
+            @pl.when(more)
+            def _():
+                pack_planes(after)
+                send_planes(after)
+            if Y > 2 * band:
+                in_line(2, X - 4, work)
 
         def step_body(step, carry):
-            @pl.when(step == 0)
-            def _():
-                set_up()
-
             def prepare():
                 @pl.when(step == 0)
                 def _():
@@ -596,10 +593,13 @@
             lax.fori_loop(1, GROUPS, group, 0)
             return carry
 
-        pack_planes(0)
-        send_beside(0)
-        pack_rows(0)
         send_across(0)
+        send_corners(0)
+        send_planes(0)
+        for there, src, dst, land, far, near, s, b in init_copies():
+            @pl.when(there)
+            def _():
+                remote(src, dst, isend.at[near], irecv.at[far], s, b).start()
         lax.fori_loop(0, STEPS, step_body, 0)
 
         result = pltpu.make_async_copy(A.at[pl.ds(2, X), rows], out.at[0], lsem.at[0])
@@ -615,8 +615,12 @@
 
         result.wait()
 
-    pl.when(is_heart)(heart_program)
-    pl.when(jnp.logical_not(is_heart))(torso_program)
+    field.wait()
+    for early in (True, False):
+        pl.when(is_heart)(functools.partial(heart_program, early))
+        pl.when(jnp.logical_not(is_heart))(functools.partial(torso_program, early))
+        if early:
+            pl.semaphore_wait(barrier, total)
 
 
 def body(mesh, potentials, coefficient, recovery, excitable, row_of):

time: 73.5 us -> 78.1 us (1.063)
  Pallas kernels: 70.8 us -> 75.4 us
    pallas_call x1, Pallas kernels: 70.8 us -> 75.4 us  [body(): pl.pallas_call(functools.partial(kernel, sections, bricks), out_shape=jax...]
where the time goes in v8:
time: 78.1 us; the launch traced here: 77.9 us
  Pallas kernels  75.4 us (97%)
  other arithmetic  1.88 us (2%)
    pallas_call x1, Pallas kernels, body(): pl.pallas_call(functools.partial(kernel, sections, bricks), out_shape=jax...  75.4 us
    mul x1, other arithmetic, body(): return fields * jnp.where(torso, PUSHES[-1], 1.0).astype(f32)  1.88 us

profile of v8, /device:TPU:0, one launch (start us, length us, event | category | flops | bytes accessed | tf_op | source)
XLA Modules:
  0.0 77.9 jit_solution(17526597341322746169)
XLA Ops:
  0.7 75.4 %shard_map.55 = f32[1,32,32,128]{3,2,1,0:T(8,128)} custom-call(f32[1,32,32,128]{3,2,1,0:T(8,128)} %pot.1, f32[1,32,32,128]{3,2,1,0:T(8,128)} %coef.1, f32[32,32,128]{2,1,0:T(8,128)} %rec.1, s32[32,32,128]{2,1,0:T(8,128)} %exc.1, s32[1]{0:T(128)S(6)} %copy.6.row_of), custom_call_target="tpu_custom_call" | custom-call | flops 50331648 | bytes 2621440 | tf_op jit(solution)/shard_map/pallas_call | solution.py:645
  76.0 1.9 %broadcast_multiply_fusion = f32[1,32,32,128]{3,2,1,0:T(8,128)} fusion(f32[1,32,32,128]{3,2,1,0:T(8,128)} %shard_map.55, f32[]{:T(128)S(6)} %select_n.4), kind=kLoop, calls=%fused_computation | loop fusion | flops 131072 | bytes 1048580 | tf_op jit(solution)/shard_map/mul | solution.py:659

commit v9 on v8

--- a/solution.py
+++ b/solution.py
@@ -313,14 +313,28 @@
                     nothing(slot, at_c[n])
 
         def send_planes(slot):
-            for i in range(2):
+            def one_side(i):
                 @pl.when(has_x[i])
                 def _():
-                    message(slot, at_x[1 - i], at_x[i], sec, to_x[i]).start()
+                    for n in range(2):
+                        message(slot, (at_x[1 - i][0] + n * Y, Y), (at_x[i][0] + n * Y, Y),
+                                sec, to_x[i]).start()
 
                 @pl.when(jnp.logical_not(has_x[i]))
                 def _():
                     nothing(slot, at_x[i])
+
+            even = lax.rem(brick, 2) == 0
+
+            @pl.when(even)
+            def _():
+                one_side(0)
+                one_side(1)
+
+            @pl.when(jnp.logical_not(even))
+            def _():
+                one_side(1)
+                one_side(0)
 
         def send_across(slot):
             for j in range(2):
@@ -479,27 +493,27 @@
             for j, at in ((0, PAD - 1), (1, PAD + Y)):
                 flat, where = across(B, at, 2, X, Y + 2 * PAD)
                 flat[where, :] = R2[j]
+            outer_planes = plane(B, A, False, weight, scale)
+            done = [outer_planes(x) for x in (0, 1, X - 2, X - 1)]
+            for value, store in done:
+                store(value)
+
+            @pl.when(more)
+            def _():
+                pack_corners(after)
+                pack_planes(after)
+                send_corners(after)
+                send_planes(after)
             band = 8 if Y > 16 else Y // 2
             for low in (0, Y - band):
-                in_line(0, X, plane(B, A, False, weight, scale, low, low + band))
+                in_line(2, X - 4, plane(B, A, False, weight, scale, low, low + band))
 
             @pl.when(more)
             def _():
                 pack_rows(after)
                 send_across(after)
-                pack_corners(after)
-                send_corners(after)
-            work = plane(B, A, False, weight, scale, band, Y - band)
             if Y > 2 * band:
-                for low in (0, X - 2):
-                    in_line(low, 2, work)
-
-            @pl.when(more)
-            def _():
-                pack_planes(after)
-                send_planes(after)
-            if Y > 2 * band:
-                in_line(2, X - 4, work)
+                in_line(2, X - 4, plane(B, A, False, weight, scale, band, Y - band))
 
         def step_body(step, carry):
             def prepare():
@@ -522,9 +536,6 @@
                 return own_v * value, store
             for_planes(0, X, 4, current)
 
-            @pl.when(inner_layer)
-            def _():
-                current_copy(step, 0, X).start()
 
             flags = [jnp.where(PR[i] == section, 1.0, 0.0) for i in range(2)]
 
@@ -558,10 +569,14 @@
                 R2[j] = R2[j] + 0.5 * BR[j]
             second_sweep(0, push[1], None, True)
 
+            @pl.when(inner_layer)
+            def _():
+                current_copy(step, 0, X).start()
+
             def group(g, carry):
                 slot = lax.rem(g, 2)
 
-                @pl.when(jnp.logical_and(g == 1, sec == heart - 2))
+                @pl.when(jnp.logical_and(g == 2, sec == heart - 2))
                 def _():
                     remote(JB.at[step, 0], JB.at[step, 0], jsend.at[step], jrecv.at[step, 0],
                            heart, brick).wait_recv()
@@ -572,9 +587,10 @@
                         return JA[step, x] + JB[step, 0, x], store
                     for_planes(0, X, 4, add)
 
-                @pl.when(jnp.logical_and(g <= pieces, jnp.logical_not(inner_layer)))
-                def _():
-                    current_copy(step, (g - 1) * piece, piece).start()
+                @pl.when(jnp.logical_and(jnp.logical_and(g >= 2, g < pieces + 2),
+                                         jnp.logical_not(inner_layer)))
+                def _():
+                    current_copy(step, (g - 2) * piece, piece).start()
 
                 @pl.when(jnp.logical_and(jnp.logical_and(g == GROUPS - 3, step + 1 < STEPS),
                                          sec == heart - 2))

time: 78.1 us -> 73.9 us (0.946)
  Pallas kernels: 75.4 us -> 71.2 us
    pallas_call x1, Pallas kernels: 75.4 us -> 71.2 us  [body(): pl.pallas_call(functools.partial(kernel, sections, bricks), out_shape=jax...]
where the time goes in v9:
time: 73.9 us; the launch traced here: 73.7 us
  Pallas kernels  71.2 us (96%)
  other arithmetic  1.88 us (3%)
    pallas_call x1, Pallas kernels, body(): pl.pallas_call(functools.partial(kernel, sections, bricks), out_shape=jax...  71.2 us
    mul x1, other arithmetic, body(): return fields * jnp.where(torso, PUSHES[-1], 1.0).astype(f32)  1.88 us

profile of v9, /device:TPU:0, one launch (start us, length us, event | category | flops | bytes accessed | tf_op | source)
XLA Modules:
  0.0 73.7 jit_solution(12334840855607695427)
XLA Ops:
  0.7 71.2 %shard_map.55 = f32[1,32,32,128]{3,2,1,0:T(8,128)} custom-call(f32[1,32,32,128]{3,2,1,0:T(8,128)} %pot.1, f32[1,32,32,128]{3,2,1,0:T(8,128)} %coef.1, f32[32,32,128]{2,1,0:T(8,128)} %rec.1, s32[32,32,128]{2,1,0:T(8,128)} %exc.1, s32[1]{0:T(128)S(6)} %copy.6.row_of), custom_call_target="tpu_custom_call" | custom-call | flops 50331648 | bytes 2621440 | tf_op jit(solution)/shard_map/pallas_call | solution.py:661
  71.9 1.9 %broadcast_multiply_fusion = f32[1,32,32,128]{3,2,1,0:T(8,128)} fusion(f32[1,32,32,128]{3,2,1,0:T(8,128)} %shard_map.55, f32[]{:T(128)S(6)} %select_n.4), kind=kLoop, calls=%fused_computation | loop fusion | flops 131072 | bytes 1048580 | tf_op jit(solution)/shard_map/mul | solution.py:675

commit v10 on v9

--- a/solution.py
+++ b/solution.py
@@ -316,9 +316,7 @@
             def one_side(i):
                 @pl.when(has_x[i])
                 def _():
-                    for n in range(2):
-                        message(slot, (at_x[1 - i][0] + n * Y, Y), (at_x[i][0] + n * Y, Y),
-                                sec, to_x[i]).start()
+                    message(slot, at_x[1 - i], at_x[i], sec, to_x[i]).start()
 
                 @pl.when(jnp.logical_not(has_x[i]))
                 def _():
@@ -421,6 +419,11 @@
                 A[j, rows, :] = H[slot, pl.ds(at_x[0][0] + j * Y, Y), :]
                 A[X + 2 + j, rows, :] = H[slot, pl.ds(at_x[1][0] + j * Y, Y), :]
                 R[j, pl.ds(PAD, X), :] = H[slot, pl.ds(at_y[j][0], X), :]
+            for j, at in ((0, PAD - 1), (1, PAD + Y)):
+                for i, x in ((0, 0), (1, X - 1)):
+                    A[x + 2, pl.ds(at, 1), :] = H[slot, pl.ds(at_y[j][0] + x, 1), :]
+                    corner = H[slot, pl.ds(at_c[2 * i + j][0], 1), :]
+                    A[1 if i == 0 else X + 2, pl.ds(at, 1), :] = corner
             for n, (i, j) in enumerate(DIAGONAL):
                 R[j, pl.ds(PAD - 1 if i == 0 else PAD + X, 1), :] = H[slot, pl.ds(at_c[n][0], 1), :]
 
@@ -438,7 +441,7 @@
             for value, store in done:
                 store(value)
             fringe(slot, first, weight)
-            mend(B, -1, X + 1, R, PAD, 0.5 if first else 1.0)
+            mend(B, 1, X - 1, R, PAD, 0.5 if first else 1.0)
 
         def relay_source(step, n):
             return source_copy(step, n, 2, heart - 3)
@@ -500,10 +503,10 @@
 
             @pl.when(more)
             def _():
+                pack_planes(after)
+                send_planes(after)
                 pack_corners(after)
-                pack_planes(after)
                 send_corners(after)
-                send_planes(after)
             band = 8 if Y > 16 else Y // 2
             for low in (0, Y - band):
                 in_line(2, X - 4, plane(B, A, False, weight, scale, low, low + band))

time: 73.9 us -> 76.2 us (1.031)
  Pallas kernels: 71.2 us -> 73.4 us
    pallas_call x1, Pallas kernels: 71.2 us -> 73.4 us  [body(): pl.pallas_call(functools.partial(kernel, sections, bricks), out_shape=jax...]
where the time goes in v10:
time: 76.2 us; the launch traced here: 76 us
  Pallas kernels  73.4 us (96%)
  other arithmetic  1.88 us (2%)
    pallas_call x1, Pallas kernels, body(): pl.pallas_call(functools.partial(kernel, sections, bricks), out_shape=jax...  73.4 us
    mul x1, other arithmetic, body(): return fields * jnp.where(torso, PUSHES[-1], 1.0).astype(f32)  1.88 us

profile of v10, /device:TPU:0, one launch (start us, length us, event | category | flops | bytes accessed | tf_op | source)
XLA Modules:
  0.0 76.0 jit_solution(2611768379036974008)
XLA Ops:
  0.7 73.4 %shard_map.55 = f32[1,32,32,128]{3,2,1,0:T(8,128)} custom-call(f32[1,32,32,128]{3,2,1,0:T(8,128)} %pot.1, f32[1,32,32,128]{3,2,1,0:T(8,128)} %coef.1, f32[32,32,128]{2,1,0:T(8,128)} %rec.1, s32[32,32,128]{2,1,0:T(8,128)} %exc.1, s32[1]{0:T(128)S(6)} %copy.6.row_of), custom_call_target="tpu_custom_call" | custom-call | flops 50331648 | bytes 2621440 | tf_op jit(solution)/shard_map/pallas_call | solution.py:664
  74.1 1.9 %broadcast_multiply_fusion = f32[1,32,32,128]{3,2,1,0:T(8,128)} fusion(f32[1,32,32,128]{3,2,1,0:T(8,128)} %shard_map.55, f32[]{:T(128)S(6)} %select_n.4), kind=kLoop, calls=%fused_computation | loop fusion | flops 131072 | bytes 1048580 | tf_op jit(solution)/shard_map/mul | solution.py:678
